TPU v7x, 32 devices: a whole 2x2x4 slice. The times are simulated.
32 devices in a mesh: seq: 8 (over z, y), fsdp: 4 (over x, core).
Axes of the slice: x: 2, y: 2, z: 4, core: 2. Of those that a mesh axis runs over, the one named last changes fastest.
Arguments:
- x_tokens: bfloat16 [5120, 5120], P('seq', 'fsdp'), may hold values from -6 to 6
- w_qkv: bfloat16 [3, 5120, 5120], P(None, 'seq', 'fsdp'), may hold values from -0.078125 to 0.078125
- q_gain: float32 [5120], P('fsdp'), may hold values from 0.5 to 6
- k_gain: float32 [5120], P('fsdp'), may hold values from 0.5 to 6
- head_kind: int32 [40], P('fsdp'), may hold values from 0 to 1, as said below
- block_live: int32 [8, 40, 5, 5], P('seq', 'fsdp'), may hold values from 0 to 1, as said below
Outputs:
- attended: bfloat16 [5120, 5120], P('seq', 'fsdp')
Inputs may be any that keep to these rules, and one draw needn't show every extreme that they name: `head_kind`: each aligned block of 10 consecutive heads holds exactly 5 heads labelled 1. block_live[f, h, i, i] is 1 for every frame, head and block i.
All inputs are finite; a program needn't handle non-finite values.
Results may differ from a plain program's by a relative error of at most 0.006.
The roundings to bfloat16 on the way count: a program that leaves them out, or rounds other values in their place, can miss the bound.
Values may be sent and summed in bfloat16 or wider, within the bound.
A program may use at most 128 MiB of HBM per device.

v0:
```python
import math

import jax
import jax.numpy as jnp
from jax import lax
from jax.sharding import PartitionSpec as P

H = 40
HD = 128
BLK = 128


def softmax_rows(scores):
    row_max = jnp.max(scores, axis=-1, keepdims=True)
    expo = jnp.exp(scores - row_max)
    return (expo / jnp.sum(expo, axis=-1, keepdims=True)).astype(jnp.bfloat16)


def spatial_attend(queries, keys_n, values, live_blocks):
    score_scale = 1.0 / math.sqrt(HD)
    scores = (
        jnp.einsum("fqhd,fkhd->fhqk", queries, keys_n, preferred_element_type=jnp.float32)
        * score_scale
    )
    key_mask = jnp.repeat(jnp.repeat(live_blocks, BLK, axis=2), BLK, axis=3)
    scores = jnp.where(key_mask, scores, -1e30)
    sp_weights = softmax_rows(scores)
    return jnp.einsum(
        "fhqk,fkhd->fqhd", sp_weights, values, preferred_element_type=jnp.float32
    ).astype(jnp.bfloat16)


def temporal_attend(triple):
    queries, keys_n, values = triple
    frame_count, single, pos_count, col_width = queries.shape
    head_count = col_width // HD
    grid_shape = (frame_count, pos_count, head_count, HD)
    score_scale = 1.0 / math.sqrt(HD)
    scores = (
        jnp.einsum(
            "fphd,gphd->phfg",
            queries.reshape(grid_shape),
            keys_n.reshape(grid_shape),
            preferred_element_type=jnp.float32,
        )
        * score_scale
    )
    tm_weights = softmax_rows(scores)
    result = jnp.einsum(
        "phfg,gphd->fphd",
        tm_weights,
        values.reshape(grid_shape),
        preferred_element_type=jnp.float32,
    )
    return result.astype(jnp.bfloat16).reshape(frame_count, single, pos_count, col_width)


def shards(x_tokens, w_qkv, q_gain, k_gain, head_kind, block_live):
    full_tokens = lax.all_gather(x_tokens, "fsdp", axis=1, tiled=True)
    tok_rows = full_tokens.shape[0]
    col_width = w_qkv.shape[2]

    def add_rows(shard_rows):
        return jnp.dot(full_tokens, shard_rows, preferred_element_type=jnp.float32)

    q_raw = add_rows(lax.all_gather(w_qkv[0], "seq", axis=0, tiled=True))
    k_raw = add_rows(lax.all_gather(w_qkv[1], "seq", axis=0, tiled=True))
    v_raw = add_rows(lax.all_gather(w_qkv[2], "seq", axis=0, tiled=True))
    q_sq, k_sq = lax.psum((jnp.sum(q_raw * q_raw, axis=1), jnp.sum(k_raw * k_raw, axis=1)), "fsdp")
    total_cols = H * HD
    queries = (q_raw * lax.rsqrt(q_sq[:, None] / total_cols + 1e-06) * q_gain).astype(jnp.bfloat16)
    keys_n = (k_raw * lax.rsqrt(k_sq[:, None] / total_cols + 1e-06) * k_gain).astype(jnp.bfloat16)
    values = v_raw.astype(jnp.bfloat16)
    seq_count = lax.axis_size("seq")
    frames_dev = block_live.shape[0]
    positions = tok_rows // frames_dev
    per_device = positions // seq_count
    head_count = col_width // HD
    live_blocks = block_live > 0

    def to_blocks(columns):
        return columns.reshape(frames_dev, seq_count, per_device, col_width)

    relayed = temporal_attend(
        (
            lax.all_to_all(to_blocks(queries), "seq", split_axis=1, concat_axis=0, tiled=True),
            lax.all_to_all(to_blocks(keys_n), "seq", split_axis=1, concat_axis=0, tiled=True),
            lax.all_to_all(to_blocks(values), "seq", split_axis=1, concat_axis=0, tiled=True),
        )
    )
    returned = lax.all_to_all(relayed, "seq", split_axis=0, concat_axis=1, tiled=True).reshape(
        tok_rows, col_width
    )
    grid_shape = (frames_dev, positions, head_count, HD)
    spatial = spatial_attend(
        queries.reshape(grid_shape),
        keys_n.reshape(grid_shape),
        values.reshape(grid_shape),
        live_blocks,
    )
    is_temporal = jnp.repeat(head_kind > 0, HD)[None, :]
    return jnp.where(is_temporal, returned, spatial.reshape(tok_rows, col_width))


def solution(mesh):
    placed = (
        P("seq", "fsdp"),
        P(None, "seq", "fsdp"),
        P("fsdp"),
        P("fsdp"),
        P("fsdp"),
        P("seq", "fsdp", None, None),
    )
    return jax.shard_map(
        shards, mesh=mesh, in_specs=placed, out_specs=P("seq", "fsdp"), check_vma=False
    )
```

profile of v0, /device:TPU:12, one launch (start us, length us, event | category | flops | bytes accessed | tf_op | source)
XLA Modules:
  0.0 800.4 jit_solution(16603312149602847531)
XLA Ops:
  7.3 4.8 fusion.27
  13.5 44.5 %all-gather.8.cloned.1.call-done = bf16[640,5120]{1,0:T(8,128)(2,1)} async-done(((bf16[640,1280]{1,0:T(8,128)(2,1)}), bf16[640,5120]{1,0:T(8,128)(2,1)}) %all-gather.8.cloned.1.call-update) | async-done | bytes 6553616 | tf_op jit(solution)/shard_map/all_gather | solution.py:59
  57.9 182.2 %all-gather.14.cloned.1.call-done = bf16[1,5120,1280]{2,1,0:T(8,128)(2,1)} async-done(((bf16[1,640,1280]{2,1,0:T(8,128)(2,1)}), bf16[1,5120,1280]{2,1,0:T(8,128)(2,1)}) %all-gather.14.cloned.1.call-update) | async-done | bytes 13107216 | tf_op jit(solution)/shard_map/all_gather | solution.py:67
  240.1 14.6 %multiply_reduce_fusion = (f32[640]{0:T(1024)S(1)}, f32[640,1280]{1,0:T(8,128)}) fusion(bf16[640,5120]{1,0:T(8,128)(2,1)} %all-gather.8.cloned.1.call-done, bf16[1,5120,1280]{2,1,0:T(8,128)(2,1)} %all-gather.14.cloned.1.call-done), kind=kOutput, calls=%fused_computation.15 | convolution fusion | flops 8390245888 | bytes 22940160 | tf_op jit(solution)/shard_map/dot_general | solution.py:64
  254.8 168.6 %all-gather.12.cloned.1.call-done = bf16[1,5120,1280]{2,1,0:T(8,128)(2,1)} async-done(((bf16[1,640,1280]{2,1,0:T(8,128)(2,1)}), bf16[1,5120,1280]{2,1,0:T(8,128)(2,1)}) %all-gather.12.cloned.1.call-update) | async-done | bytes 13107216 | tf_op jit(solution)/shard_map/all_gather | solution.py:66
  423.4 12.9 %multiply_reduce_fusion.1 = (f32[640]{0:T(1024)S(1)}, f32[640,1280]{1,0:T(8,128)S(1)}) fusion(bf16[640,5120]{1,0:T(8,128)(2,1)} %all-gather.8.cloned.1.call-done, bf16[1,5120,1280]{2,1,0:T(8,128)(2,1)} %all-gather.12.cloned.1.call-done), kind=kOutput, calls=%fused_computation.17 | convolution fusion | flops 8390245888 | bytes 22940160 | tf_op jit(solution)/shard_map/dot_general | solution.py:64
  436.3 6.7 all-reduce
  444.7 6.8 all-to-all-start.1
  451.5 3.5 multiply_convert_fusion
  455.0 67.7 %all-to-all-done.1 = bf16[1,8,80,1280]{3,2,0,1:T(8,128)(2,1)S(1)} async-done(((bf16[1,8,80,1280]{3,2,0,1:T(8,128)(2,1)}), bf16[1,8,80,1280]{3,2,0,1:T(8,128)(2,1)S(1)}, u32[]{:S(2)}, u32[]{:S(2)}) %all-to-all-start.1) | async-done | bytes 1638432 | tf_op jit(solution)/shard_map/all_to_all | solution.py:86
  522.7 7.8 all-to-all-start.2
  530.5 140.7 %all-gather.10.cloned.1.call-done = bf16[1,5120,1280]{2,1,0:T(8,128)(2,1)} async-done(((bf16[1,640,1280]{2,1,0:T(8,128)(2,1)}), bf16[1,5120,1280]{2,1,0:T(8,128)(2,1)}) %all-gather.10.cloned.1.call-update) | async-done | bytes 13107216 | tf_op jit(solution)/shard_map/all_gather | solution.py:68
  671.1 14.0 %fusion.9 = bf16[640,1280]{1,0:T(8,128)(2,1)} fusion(bf16[640,5120]{1,0:T(8,128)(2,1)} %all-gather.8.cloned.1.call-done, bf16[1,5120,1280]{2,1,0:T(8,128)(2,1)} %all-gather.10.cloned.1.call-done), kind=kOutput, calls=%fused_computation.18 | convolution fusion | flops 8389427200 | bytes 21299200 | tf_op jit(solution)/shard_map/dot_general | solution.py:64
  686.3 8.0 all-to-all-start
  697.1 4.2 reshape.103
  701.3 3.7 fusion.17
  705.0 3.2 fusion.29
  708.2 21.7 %all-to-all-done = bf16[1,8,80,1280]{3,2,0,1:T(8,128)(2,1)} async-done(((bf16[1,8,80,1280]{3,2,0,1:T(8,128)(2,1)}), bf16[1,8,80,1280]{3,2,0,1:T(8,128)(2,1)}, u32[]{:S(2)}, u32[]{:S(2)}) %all-to-all-start) | async-done | bytes 1638432 | tf_op jit(solution)/shard_map/all_to_all | solution.py:88
  732.7 3.0 fusion.22
  738.5 7.6 all-to-all-start.3
  752.3 3.5 copy.36
  755.8 6.9 multiply_select_fusion
  762.7 12.8 %fusion.28 = f32[10,640]{1,0:T(8,128)S(1)} fusion(f32[10,640,640]{1,2,0:T(8,128)} %multiply_select_fusion), kind=kOutput, calls=%fused_computation.39 | output fusion | flops 8192639 | bytes 16409600 | tf_op jit(solution)/shard_map/sub | solution.py:15
  775.5 14.4 %fusion.15 = bf16[10,128,640]{2,1,0:T(8,128)(2,1)S(1)} fusion(bf16[640,10,128]{0,2,1:T(8,128)(2,1)S(1)} %bitcast.67, f32[10,640]{1,0:T(8,128)S(1)} %fusion.28, f32[10,640,640]{1,2,0:T(8,128)} %multiply_select_fusion), kind=kOutput, calls=%fused_computation.22 | convolution fusion | flops 1061690240 | bytes 19686400 | tf_op jit(solution)/shard_map/fhqk,fkhd->fqhd/dot_general | solution.py:28
  (40 shorter events, 23.3 us)
Async XLA Ops:
  6.5 51.4 %all-gather.8.cloned.1.call-start = ((), (), s32[]{:S(2)}) async-start(), calls=%async_computation.4 | async-start | bytes 8192000 | tf_op jit(solution)/shard_map/all_gather | solution.py:59
  7.3 232.9 %all-gather.14.cloned.1.call-start = ((), (), s32[]{:S(2)}) async-start(), calls=%async_computation.7 | async-start | bytes 14745600 | tf_op jit(solution)/shard_map/all_gather | solution.py:67
  12.1 411.3 %all-gather.12.cloned.1.call-start = ((), (), s32[]{:S(2)}) async-start(), calls=%async_computation.6 | async-start | bytes 14745600 | tf_op jit(solution)/shard_map/all_gather | solution.py:66
  12.9 658.3 %all-gather.10.cloned.1.call-start = ((), (), s32[]{:S(2)}) async-start(), calls=%async_computation.5 | async-start | bytes 14745600 | tf_op jit(solution)/shard_map/all_gather | solution.py:68
  254.8 188.3 %copy-start.4 = (f32[1280]{0:T(1024)S(1)}, f32[1280]{0:T(1024)}, u32[]{:S(2)}) copy-start(f32[1280]{0:T(1024)} %param.8) | copy-start | bytes 15364
  443.1 8.3 %copy-start.5 = (f32[1280]{0:T(1024)S(1)}, f32[1280]{0:T(1024)}, u32[]{:S(2)}) copy-start(f32[1280]{0:T(1024)} %param.9) | copy-start | bytes 15364
  444.7 78.0 %all-to-all-start.1 = ((bf16[1,8,80,1280]{3,2,0,1:T(8,128)(2,1)}), bf16[1,8,80,1280]{3,2,0,1:T(8,128)(2,1)S(1)}, u32[]{:S(2)}, u32[]{:S(2)}) async-start(bf16[1,8,80,1280]{3,2,0,1:T(8,128)(2,1)} %bitcast.6), calls=%async_computation.1 | async-start | bytes 3276800 | tf_op jit(solution)/shard_map/all_to_all | solution.py:86
  522.7 162.4 %copy-start = (bf16[1,8,80,1280]{3,2,0,1:T(8,128)(2,1)}, bf16[1,8,80,1280]{3,2,0,1:T(8,128)(2,1)S(1)}, u32[]{:S(2)}) copy-start(bf16[1,8,80,1280]{3,2,0,1:T(8,128)(2,1)S(1)} %all-to-all-done.1) | copy-start | bytes 4915204
  522.7 162.5 %all-to-all-start.2 = ((bf16[1,8,80,1280]{3,2,0,1:T(8,128)(2,1)}), bf16[1,8,80,1280]{3,2,0,1:T(8,128)(2,1)S(1)}, u32[]{:S(2)}, u32[]{:S(2)}) async-start(bf16[1,8,80,1280]{3,2,0,1:T(8,128)(2,1)} %bitcast.9), calls=%async_computation.2 | async-start | bytes 3276800 | tf_op jit(solution)/shard_map/all_to_all | solution.py:87
  685.1 1.2 copy-start.1
  686.3 43.6 %all-to-all-start = ((bf16[1,8,80,1280]{3,2,0,1:T(8,128)(2,1)}), bf16[1,8,80,1280]{3,2,0,1:T(8,128)(2,1)}, u32[]{:S(2)}, u32[]{:S(2)}) async-start(bf16[1,8,80,1280]{3,2,0,1:T(8,128)(2,1)} %bitcast.3), calls=%async_computation | async-start | bytes 3276800 | tf_op jit(solution)/shard_map/all_to_all | solution.py:88
  736.1 10.0 %copy-start.3 = (s32[1,10,5,5]{1,0,3,2:T(1,128)S(1)}, s32[1,10,5,5]{1,0,3,2:T(1,128)}, u32[]{:S(2)}) copy-start(s32[1,10,5,5]{1,0,3,2:T(1,128)} %param.11) | copy-start | bytes 3004
  736.1 10.3 %copy-start.6 = (s32[10]{0:T(128)S(1)}, s32[10]{0:T(128)}, u32[]{:S(2)}) copy-start(s32[10]{0:T(128)} %param.10) | copy-start | bytes 124
  738.5 52.7 %all-to-all-start.3 = ((bf16[8,1,80,1280]{3,2,1,0:T(8,128)(2,1)}), bf16[8,1,80,1280]{3,2,1,0:T(8,128)(2,1)}, u32[]{:S(2)}, u32[]{:S(2)}) async-start(bf16[8,1,80,1280]{3,2,1,0:T(8,128)(2,1)} %bitcast.66), calls=%async_computation.3 | async-start | bytes 3276800 | tf_op jit(solution)/shard_map/all_to_all | solution.py:91
  762.7 12.8 %copy-start.2 = (bf16[640,1280]{0,1:T(8,128)(2,1)S(1)}, bf16[640,1280]{0,1:T(8,128)(2,1)}, u32[]{:S(2)}) copy-start(bf16[640,1280]{0,1:T(8,128)(2,1)} %copy.36) | copy-start | bytes 4915204
Sparse Core Ops, SparseCore 0:
  8.9 48.9 all-gather.7
  60.1 179.9 all-gather.13
  242.3 180.9 all-gather.11
  425.4 245.6 all-gather.9
where the time goes:
time: 803 us; the launch traced here: 800 us
  waiting for transfers between devices  627 us (78%)
  matrix products  69.5 us (9%)
  starting transfers between devices  30.3 us (4%)
  local copies, waits for them, and re-layouts  29.5 us (4%)
  other arithmetic  23.8 us (3%)
  between operations  13.3 us (2%)
    all_gather x1, waiting for transfers between devices, shards(): k_raw = add_rows(lax.all_gather(w_qkv[1], 'seq', axis=0, tiled=True))  182 us
    all_gather x1, waiting for transfers between devices, shards(): q_raw = add_rows(lax.all_gather(w_qkv[0], 'seq', axis=0, tiled=True))  169 us
    all_gather x1, waiting for transfers between devices, shards(): v_raw = add_rows(lax.all_gather(w_qkv[2], 'seq', axis=0, tiled=True))  141 us
    all_to_all x1, waiting for transfers between devices, shards(): lax.all_to_all(to_blocks(queries), 'seq', split_axis=1, concat_axis=0, ti...  67.7 us
    all_gather x1, waiting for transfers between devices, shards(): full_tokens = lax.all_gather(x_tokens, 'fsdp', axis=1, tiled=True)  44.5 us
    dot_general x3, matrix products, add_rows(): return jnp.dot(full_tokens, shard_rows, preferred_element_type=jnp.float32)  41.5 us
    all_to_all x1, waiting for transfers between devices, shards(): lax.all_to_all(to_blocks(values), 'seq', split_axis=1, concat_axis=0, til...  21.7 us
  transfers between devices with their start and end apart: 8, of which 6 were waited for; matrix products, arithmetic and copies ran while one was open for 14% of the time, Pallas kernels for 0%

commit v1 on v0

--- a/solution.py
+++ b/solution.py
@@ -3,6 +3,8 @@
 import jax
 import jax.numpy as jnp
 from jax import lax
+from jax.experimental import pallas as pl
+from jax.experimental.pallas import tpu as pltpu
 from jax.sharding import PartitionSpec as P
 
 H = 40
@@ -101,6 +103,223 @@
     is_temporal = jnp.repeat(head_kind > 0, HD)[None, :]
     return jnp.where(is_temporal, returned, spatial.reshape(tok_rows, col_width))
 
+def attend_kernel(role_ref, bias_ref, q_ref, k_ref, v_ref, out_ref):
+    head = pl.program_id(0)
+    score_scale = 1.0 / math.sqrt(HD)
+    slots, quarter, _ = q_ref.shape
+    frame_slots = slots // 2
+    frame_rows = frame_slots * quarter
+    blocks = frame_rows // BLK
+    contract_last = (((1,), (1,)), ((), ()))
+
+    def weigh(scores, vals):
+        row_max = jnp.max(scores, axis=-1, keepdims=True)
+        expo = jnp.exp(scores - row_max)
+        weights = (expo * (1.0 / jnp.sum(expo, axis=-1, keepdims=True))).astype(jnp.bfloat16)
+        return jnp.dot(weights, vals, preferred_element_type=jnp.float32).astype(jnp.bfloat16)
+
+    @pl.when(role_ref[0] == 1)
+    def _():
+        for frame in range(2):
+            at = pl.ds(frame * frame_slots, frame_slots)
+            qs = q_ref[at].reshape(frame_rows, HD)
+            ks = k_ref[at].reshape(frame_rows, HD)
+            vs = v_ref[at].reshape(frame_rows, HD)
+            pieces = []
+            for qb in range(blocks):
+                scores = (
+                    lax.dot_general(
+                        qs[qb * BLK : (qb + 1) * BLK],
+                        ks,
+                        contract_last,
+                        preferred_element_type=jnp.float32,
+                    )
+                    * score_scale
+                )
+                masked = [
+                    scores[:, kb * BLK : (kb + 1) * BLK]
+                    + bias_ref[frame, head, qb * blocks + kb]
+                    for kb in range(blocks)
+                ]
+                pieces.append(weigh(jnp.concatenate(masked, axis=1), vs))
+            out_ref[at] = jnp.concatenate(pieces, axis=0).reshape(frame_slots, quarter, HD)
+
+    @pl.when(role_ref[0] == 0)
+    def _():
+        step = 32
+        rows = slots * step
+        row_pos = lax.broadcasted_iota(jnp.int32, (rows, rows), 0) % step
+        col_pos = lax.broadcasted_iota(jnp.int32, (rows, rows), 1) % step
+        same = row_pos == col_pos
+        for pb in range(quarter // step):
+            at = pl.ds(pb * step, step)
+            qs = q_ref[:, at].reshape(rows, HD)
+            ks = k_ref[:, at].reshape(rows, HD)
+            vs = v_ref[:, at].reshape(rows, HD)
+            scores = (
+                lax.dot_general(qs, ks, contract_last, preferred_element_type=jnp.float32)
+                * score_scale
+            )
+            res = weigh(jnp.where(same, scores, -1e30), vs)
+            out_ref[:, at] = res.reshape(slots, step, HD)
+
+
+def attend(role, bias, queries, keys_n, values):
+    slots, quarter, cols = queries.shape
+    spec = pl.BlockSpec((slots, quarter, HD), lambda h: (0, 0, h))
+    return pl.pallas_call(
+        attend_kernel,
+        grid=(cols // HD,),
+        out_shape=jax.ShapeDtypeStruct(queries.shape, jnp.bfloat16),
+        in_specs=[
+            pl.BlockSpec(memory_space=pltpu.SMEM),
+            pl.BlockSpec(memory_space=pltpu.SMEM),
+            spec,
+            spec,
+            spec,
+        ],
+        out_specs=spec,
+        compiler_params=pltpu.CompilerParams(vmem_limit_bytes=40 * 1024 * 1024),
+    )(role, bias, queries, keys_n, values)
+
+
+def pick_heads(array, heads):
+    return jnp.concatenate(
+        [lax.dynamic_slice_in_dim(array, head * HD, HD, axis=array.ndim - 1) for head in heads],
+        axis=-1,
+    )
+
+
+def along_z(shift, froms):
+    return [(2 * z + y, 2 * (z + shift) + y) for z in froms for y in range(2)]
+
+
+def split_shards(x_tokens, w_qkv, q_gain, k_gain, head_kind, block_live):
+    seq_count = lax.axis_size("seq")
+    half = seq_count // 2
+    me = lax.axis_index("seq")
+    z, y = me // 2, me % 2
+    is_spatial = me < half
+    rows, feats = x_tokens.shape
+    quarter = rows // half
+    head_count = head_kind.shape[0]
+    kept = head_count // 2
+    order = jnp.argsort(head_kind, stable=True)
+    sp_heads = [order[i] for i in range(kept)]
+    tm_heads = [order[kept + i] for i in range(kept)]
+    my_heads = [jnp.where(is_spatial, s, t) for s, t in zip(sp_heads, tm_heads)]
+
+    up_half = [(i + half, i) for i in range(half)]
+    second = lax.ppermute(x_tokens, "seq", up_half)
+    grid = x_tokens.reshape(half, quarter, feats)
+    parts = [lax.dynamic_index_in_dim(grid, jnp.maximum(me - half, 0), 0)]
+    for r in range(1, seq_count):
+        target = (me - r) % seq_count
+        block = lax.dynamic_index_in_dim(grid, jnp.maximum(target - half, 0), 0)
+        parts.append(
+            lax.ppermute(
+                block, "seq", [((d + r) % seq_count, d) for d in range(half, seq_count)]
+            )
+        )
+    mine = jnp.where(
+        is_spatial,
+        jnp.concatenate([grid, second.reshape(grid.shape)], axis=0),
+        jnp.concatenate(parts, axis=0),
+    ).reshape(2 * rows, feats)
+    hf = feats // 2
+    mine = jnp.where(y == 0, mine, jnp.concatenate([mine[:, hf:], mine[:, :hf]], axis=1))
+    feats_of = lax.all_gather(mine, "fsdp", axis=0, tiled=False)
+
+    w_sp, w_tm = pick_heads(w_qkv, sp_heads), pick_heads(w_qkv, tm_heads)
+    swap_y = [(i, i ^ 1) for i in range(seq_count)]
+    turn = jnp.where(is_spatial, 1, -1)
+    at_z = [z, z + turn, z + 2 * turn, jnp.where(z % 2 == 0, 3, 0)]
+
+    def gather_rows(sp, tm):
+        own = jnp.where(is_spatial, sp, tm)
+        down = lax.ppermute(sp, "seq", along_z(-1, (1, 2, 3)))
+        up = lax.ppermute(tm, "seq", along_z(1, (0, 1, 2)))
+        near = jnp.where(is_spatial, down, up)
+        down2 = lax.ppermute(down, "seq", along_z(-1, (1, 2)))
+        up2 = lax.ppermute(up, "seq", along_z(1, (1, 2)))
+        far = jnp.where(is_spatial, down2, up2)
+        last = lax.ppermute(
+            jnp.where((z == 0) | (z == 3), own, far),
+            "seq",
+            along_z(1, (0, 2)) + along_z(-1, (1, 3)),
+        )
+        held = [own, near, far, last]
+        return [(piece, lax.ppermute(piece, "seq", swap_y)) for piece in held]
+
+    def project(pieces, count):
+        totals = [None] * count
+        for z_at, (own, other) in zip(at_z, pieces):
+            feat = lax.dynamic_index_in_dim(feats_of, z_at, 0, keepdims=False)
+            for part, rows_w in ((feat[:, :hf], own), (feat[:, hf:], other)):
+                for i in range(count):
+                    term = jnp.dot(part, rows_w[i], preferred_element_type=jnp.float32)
+                    totals[i] = term if totals[i] is None else totals[i] + term
+        return totals
+
+    q_raw, k_raw = project(gather_rows(w_sp[:2], w_tm[:2]), 2)
+    (v_raw,) = project(gather_rows(w_sp[2:], w_tm[2:]), 1)
+
+    sq = jnp.stack([jnp.sum(q_raw * q_raw, axis=1), jnp.sum(k_raw * k_raw, axis=1)])
+    blank = jnp.zeros((2, seq_count, rows), jnp.float32)
+    sq_sp = sq.reshape(2, 2, rows)
+    of_sp = lax.dynamic_update_slice(blank, sq_sp[:, :1], (0, me % half, 0))
+    of_sp = lax.dynamic_update_slice(of_sp, sq_sp[:, 1:], (0, me % half + half, 0))
+    frame_at = (jnp.arange(seq_count) - me) % seq_count
+    pos_at = jnp.maximum(me - half, 0) * quarter
+    of_tm = lax.dynamic_update_slice(
+        blank, jnp.take(sq.reshape(2, seq_count, quarter), frame_at, axis=1), (0, 0, pos_at)
+    )
+    sums = lax.psum(jnp.where(is_spatial, of_sp, of_tm), ("seq", "fsdp"))
+    sums_sp = jnp.concatenate(
+        [
+            lax.dynamic_slice(sums, (0, me % half, 0), (2, 1, rows)),
+            lax.dynamic_slice(sums, (0, me % half + half, 0), (2, 1, rows)),
+        ],
+        axis=1,
+    ).reshape(2, 2 * rows)
+    slot_at = (jnp.arange(seq_count) + me) % seq_count
+    sums_tm = jnp.take(
+        lax.dynamic_slice(sums, (0, 0, pos_at), (2, seq_count, quarter)), slot_at, axis=1
+    ).reshape(2, 2 * rows)
+    my_sums = jnp.where(is_spatial, sums_sp, sums_tm)
+
+    def normed(raw, total, gain):
+        gains = pick_heads(gain, my_heads)
+        scaled = raw * lax.rsqrt(total[:, None] / (H * HD) + 1e-06) * gains
+        return scaled.astype(jnp.bfloat16).reshape(seq_count, quarter, kept * HD)
+
+    queries = normed(q_raw, my_sums[0], q_gain)
+    keys_n = normed(k_raw, my_sums[1], k_gain)
+    values = v_raw.astype(jnp.bfloat16).reshape(seq_count, quarter, kept * HD)
+
+    live = block_live[0]
+    live_two = jnp.stack([live, lax.ppermute(live, "seq", up_half)])
+    live_two = jnp.take(live_two, order[:kept], axis=1)
+    bias = jnp.where(live_two.reshape(2, kept, -1) > 0, 0.0, -1e30).astype(jnp.float32)
+    role = is_spatial.astype(jnp.int32).reshape(1)
+    done = attend(role, bias, queries, keys_n, values)
+
+    back = lax.ppermute(done[half:], "seq", [(i, i + half) for i in range(half)])
+    spatial = jnp.where(is_spatial, done[:half], back).reshape(rows, kept * HD)
+    came = [done[:1]]
+    for r in range(1, seq_count):
+        came.append(
+            lax.ppermute(
+                done[r : r + 1], "seq", [(s, (s + r) % seq_count) for s in range(half, seq_count)]
+            )
+        )
+    came = jnp.concatenate(came, axis=0)
+    came_at = (me - half - jnp.arange(half)) % seq_count
+    temporal = jnp.take(came, came_at, axis=0).reshape(rows, kept * HD)
+    both = jnp.concatenate([spatial, temporal], axis=1)
+    place = jnp.argsort(order)
+    return pick_heads(both, [place[h] for h in range(head_count)])
+
 
 def solution(mesh):
     placed = (
@@ -111,6 +330,18 @@
         P("fsdp"),
         P("seq", "fsdp", None, None),
     )
+
+    def chosen(x_tokens, w_qkv, q_gain, k_gain, head_kind, block_live):
+        fits = (
+            mesh.shape["seq"] == 8
+            and head_kind.shape[0] == 10
+            and block_live.shape[0] == 1
+            and x_tokens.shape[1] * mesh.shape["fsdp"] == w_qkv.shape[1] * mesh.shape["seq"]
+            and mesh.shape["fsdp"] == 4
+        )
+        body = split_shards if fits else shards
+        return body(x_tokens, w_qkv, q_gain, k_gain, head_kind, block_live)
+
     return jax.shard_map(
-        shards, mesh=mesh, in_specs=placed, out_specs=P("seq", "fsdp"), check_vma=False
-    )
+        chosen, mesh=mesh, in_specs=placed, out_specs=P("seq", "fsdp"), check_vma=False
+    )

time: 803 us -> 631 us (0.79)
  waiting for transfers between devices: 627 us -> 249 us
  starting transfers between devices: 30.3 us -> 124 us
  blocking collectives: 6.74 us -> 45.8 us
  local copies, waits for them, and re-layouts: 29.5 us -> 54.9 us
  Pallas kernels: 0 us -> 22.2 us
  between operations: 13.3 us -> 33.9 us
    all_gather x4 -> x1, waiting for transfers between devices: 536 us -> 0.01 us  [split_shards(): feats_of = lax.all_gather(mine, 'fsdp', axis=0, tiled=False)]
    ppermute x0 -> x35, waiting for transfers between devices: none -> 249 us  [the longest x8 156 us: gather_rows(): return [(piece, lax.ppermute(piece, 'seq', swap_y)) for piece in held]]
    ppermute x0 -> x35, starting transfers between devices: none -> 124 us  [the longest x7 58.9 us: split_shards(): lax.ppermute(block, 'seq', [((d + r) % seq_count, d) for d in range(half,...]
    all_to_all x4 -> x0, waiting for transfers between devices: 89.4 us -> none  [the longest x1 67.7 us: shards(): lax.all_to_all(to_blocks(queries), 'seq', split_axis=1, concat_axis=0, ti...]
    psum x1, blocking collectives: 6.74 us -> 45.8 us  [split_shards(): sums = lax.psum(jnp.where(is_spatial, of_sp, of_tm), ('seq', 'fsdp'))]
    all_to_all x4 -> x0, starting transfers between devices: 30.2 us -> none  [the longest x1 7.97 us: shards(): lax.all_to_all(to_blocks(values), 'seq', split_axis=1, concat_axis=0, til...]
    unnamed x14 -> x65, local copies, waits for them, and re-layouts: 1.21 us -> 29.7 us
    pallas_call x0 -> x1, Pallas kernels: none -> 22.2 us  [attend(): pl.pallas_call(attend_kernel, grid=(cols // HD,), out_shape=jax.ShapeDtyp...]
  transfers between devices with their start and end apart: 8 -> 36, of which waited for: 6 -> 15; matrix products, arithmetic and copies ran while one was open for 14% -> 21% of each run, Pallas kernels for 0% -> 0%
where the time goes in v1:
time: 631 us; the launch traced here: 621 us
  waiting for transfers between devices  249 us (39%)
  starting transfers between devices  124 us (20%)
  matrix products  72.2 us (11%)
  local copies, waits for them, and re-layouts  54.9 us (9%)
  blocking collectives  45.8 us (7%)
  between operations  33.9 us (5%)
  Pallas kernels  22.2 us (4%)
  other arithmetic  19.5 us (3%)
    ppermute x8, waiting for transfers between devices, gather_rows(): return [(piece, lax.ppermute(piece, 'seq', swap_y)) for piece in held]  156 us
    dot_general x24, matrix products, project(): term = jnp.dot(part, rows_w[i], preferred_element_type=jnp.float32)  72.2 us
    ppermute x7, starting transfers between devices, split_shards(): lax.ppermute(block, 'seq', [((d + r) % seq_count, d) for d in range(half,...  58.9 us
    psum x1, blocking collectives, split_shards(): sums = lax.psum(jnp.where(is_spatial, of_sp, of_tm), ('seq', 'fsdp'))  45.8 us
    ppermute x2, waiting for transfers between devices, gather_rows(): down2 = lax.ppermute(down, 'seq', along_z(-1, (1, 2)))  34.6 us
    unnamed x65, local copies, waits for them, and re-layouts  29.7 us
    ppermute x7, waiting for transfers between devices, split_shards(): lax.ppermute(done[r:r + 1], 'seq', [(s, (s + r) % seq_count) for s in ran...  23.1 us
    pallas_call x1, Pallas kernels, attend(): pl.pallas_call(attend_kernel, grid=(cols // HD,), out_shape=jax.ShapeDtyp...  22.2 us
  transfers between devices with their start and end apart: 36, of which 15 were waited for; matrix products, arithmetic and copies ran while one was open for 21% of the time, Pallas kernels for 0%

profile of v1, /device:TPU:12, one launch (start us, length us, event | category | flops | bytes accessed | tf_op | source)
XLA Modules:
  0.0 621.4 jit_solution(17923977962123035620)
XLA Ops:
  6.5 4.1 constant_dynamic-slice_fusion.3
  16.1 14.0 %collective-permute-start.5 = (bf16[1,160,1280]{2,1,0:T(8,128)(2,1)}, bf16[1,160,1280]{2,1,0:T(8,128)(2,1)}, u32[]{:S(2)}, u32[]{:S(2)}) collective-permute-start(bf16[1,160,1280]{2,1,0:T(8,128)(2,1)} %get-tuple-element.47), channel_id=1, source_target_pairs={{0,16},{4,20},{8,24},{12,28},{1,17},{5,21},{9,25},{13,29},{2,18},{... | collective-permute-start | bytes 1228808 | tf_op jit(solution)/shard_map/ppermute | solution.py:220
  36.4 38.1 %collective-permute-start.8 = (bf16[1,160,1280]{2,1,0:T(8,128)(2,1)}, bf16[1,160,1280]{2,1,0:T(8,128)(2,1)S(1)}, u32[]{:S(2)}, u32[]{:S(2)}) collective-permute-start(bf16[1,160,1280]{2,1,0:T(8,128)(2,1)} %get-tuple-element.44), channel_id=1, source_target_pairs={{12,16},{16,20},{20,24},{24,28},{13,17},{17,21},{21,25},{25,29},{1... | collective-permute-start | bytes 1228808 | tf_op jit(solution)/shard_map/ppermute | solution.py:220
  80.8 7.9 %collective-permute-done.8 = bf16[1,160,1280]{2,1,0:T(8,128)(2,1)S(1)} collective-permute-done((bf16[1,160,1280]{2,1,0:T(8,128)(2,1)}, bf16[1,160,1280]{2,1,0:T(8,128)(2,1)S(1)}, u32[]{:S(2)}, u32[]{:S(2)}) %collective-permute-start.8) | collective-permute-done | bytes 409632 | tf_op jit(solution)/shard_map/ppermute | solution.py:220
  109.7 7.1 %collective-permute-start.19 = (bf16[1,640,640]{2,1,0:T(8,128)(2,1)S(1)}, bf16[1,640,640]{2,1,0:T(8,128)(2,1)}, u32[]{:S(2)}, u32[]{:S(2)}) collective-permute-start(bf16[1,640,640]{2,1,0:T(8,128)(2,1)S(1)} %slice.308), channel_id=1, source_target_pairs={{8,0},{12,4},{16,8},{20,12},{24,16},{28,20},{9,1},{13,5},{17,9},{2... | collective-permute-start | bytes 2457608 | tf_op jit(solution)/shard_map/ppermute | solution.py:240
  121.0 4.9 collective-permute-start.10
  151.1 18.2 %collective-permute-done.10 = bf16[2,640,640]{2,1,0:T(8,128)(2,1)} collective-permute-done((bf16[2,640,640]{2,1,0:T(8,128)(2,1)}, bf16[2,640,640]{2,1,0:T(8,128)(2,1)}, u32[]{:S(2)}, u32[]{:S(2)}) %collective-permute-start.10) | collective-permute-done | bytes 1638432 | tf_op jit(solution)/shard_map/ppermute | solution.py:240
  173.5 4.1 collective-permute-start.14
  180.2 4.9 collective-permute-start.23
  189.3 34.6 %collective-permute-done.22 = bf16[1,640,640]{2,1,0:T(8,128)(2,1)S(1)} collective-permute-done((bf16[1,640,640]{2,1,0:T(8,128)(2,1)}, bf16[1,640,640]{2,1,0:T(8,128)(2,1)S(1)}, u32[]{:S(2)}, u32[]{:S(2)}) %collective-permute-start.22) | collective-permute-done | bytes 819232 | tf_op jit(solution)/shard_map/ppermute | solution.py:243
  233.8 4.1 broadcast_select_fusion
  241.9 5.4 dynamic-slice_bitcast_fusion.3
  250.8 4.5 fusion.44
  255.3 15.5 %collective-permute-done.12 = bf16[2,640,640]{2,1,0:T(8,128)(2,1)} collective-permute-done((bf16[2,640,640]{2,1,0:T(8,128)(2,1)}, bf16[2,640,640]{2,1,0:T(8,128)(2,1)}, u32[]{:S(2)}, u32[]{:S(2)}) %collective-permute-start.12) | collective-permute-done | bytes 1638432 | tf_op jit(solution)/shard_map/ppermute | solution.py:252
  275.6 4.2 collective-permute-done.16
  286.2 19.7 %collective-permute-done.9 = bf16[2,640,640]{2,1,0:T(8,128)(2,1)} collective-permute-done((bf16[2,640,640]{2,1,0:T(8,128)(2,1)}, bf16[2,640,640]{2,1,0:T(8,128)(2,1)}, u32[]{:S(2)}, u32[]{:S(2)}) %collective-permute-start.9) | collective-permute-done | bytes 1638432 | tf_op jit(solution)/shard_map/ppermute | solution.py:252
  310.8 30.2 %collective-permute-done.15 = bf16[2,640,640]{2,1,0:T(8,128)(2,1)} collective-permute-done((bf16[2,640,640]{2,1,0:T(8,128)(2,1)}, bf16[2,640,640]{2,1,0:T(8,128)(2,1)}, u32[]{:S(2)}, u32[]{:S(2)}) %collective-permute-start.15) | collective-permute-done | bytes 1638432 | tf_op jit(solution)/shard_map/ppermute | solution.py:252
  351.3 91.0 %collective-permute-done.17 = bf16[2,640,640]{2,1,0:T(8,128)(2,1)S(1)} collective-permute-done((bf16[2,640,640]{2,1,0:T(8,128)(2,1)}, bf16[2,640,640]{2,1,0:T(8,128)(2,1)S(1)}, u32[]{:S(2)}, u32[]{:S(2)}) %collective-permute-start.17) | collective-permute-done | bytes 1638432 | tf_op jit(solution)/shard_map/ppermute | solution.py:252
  468.6 45.8 %psum.7 = f32[2,8,640]{2,0,1:T(2,128)S(1)} all-reduce(f32[2,8,640]{2,0,1:T(2,128)S(1)} %bitcast.155), channel_id=1, replica_groups=mesh['seq'=8,'fsdp'=4] {'seq','fsdp'}, use_global_device_ids=true, to_apply=%region_3.5 | all-reduce | flops 10240 | bytes 81920 | tf_op jit(solution)/shard_map/psum | solution.py:277
  542.3 22.2 %shard_map.64 = bf16[8,160,640]{2,1,0:T(8,128)(2,1)S(1)} custom-call(s32[1]{0:T(128)} %bitcast.role_ref, f32[2,5,25]{2,1,0:T(8,128)S(1)} %fusion.74.bias_ref, bf16[8,160,640]{2,1,0:T(8,128)(2,1)S(1)} %bitcast.137, bf16[8,160,640]{2,1,0:T(8,128)(2,1)S(1)} %bitcast.136, bf16[8,160,640]{2,1,0:T(8,128)(2,1)S(1)} %bitcast.138), custom_call_target="tpu_custom_call" | custom-call | tf_op jit(solution)/shard_map/pallas_call | solution.py:170
  566.8 8.3 %collective-permute-start.27 = (bf16[4,160,640]{2,1,0:T(8,128)(2,1)S(1)}, bf16[4,160,640]{2,1,0:T(8,128)(2,1)}, u32[]{:S(2)}, u32[]{:S(2)}) collective-permute-start(bf16[4,160,640]{2,1,0:T(8,128)(2,1)S(1)} %slice.311), channel_id=1, source_target_pairs={{0,16},{4,20},{8,24},{12,28},{1,17},{5,21},{9,25},{13,29},{2,18},{... | collective-permute-start | bytes 2457608 | tf_op jit(solution)/shard_map/ppermute | solution.py:307
  583.0 6.6 %collective-permute-done.31 = bf16[1,160,640]{2,1,0:T(8,128)(2,1)S(1)} collective-permute-done((bf16[1,160,640]{2,1,0:T(8,128)(2,1)S(1)}, bf16[1,160,640]{2,1,0:T(8,128)(2,1)S(1)}, u32[]{:S(2)}, u32[]{:S(2)}) %collective-permute-start.31) | collective-permute-done | bytes 204832 | tf_op jit(solution)/shard_map/ppermute | solution.py:312
  590.3 6.3 %collective-permute-done.32 = bf16[1,160,640]{2,1,0:T(8,128)(2,1)S(1)} collective-permute-done((bf16[1,160,640]{2,1,0:T(8,128)(2,1)S(1)}, bf16[1,160,640]{2,1,0:T(8,128)(2,1)S(1)}, u32[]{:S(2)}, u32[]{:S(2)}) %collective-permute-start.32) | collective-permute-done | bytes 204832 | tf_op jit(solution)/shard_map/ppermute | solution.py:312
  597.3 7.6 %collective-permute-done.33 = bf16[1,160,640]{2,1,0:T(8,128)(2,1)S(1)} collective-permute-done((bf16[1,160,640]{2,1,0:T(8,128)(2,1)S(1)}, bf16[1,160,640]{2,1,0:T(8,128)(2,1)S(1)}, u32[]{:S(2)}, u32[]{:S(2)}) %collective-permute-start.33) | collective-permute-done | bytes 204832 | tf_op jit(solution)/shard_map/ppermute | solution.py:312
  (224 shorter events, 178.3 us)
Async XLA Ops:
  6.5 235.4 %all-gather.2.cloned.1.call-start = ((), (), s32[]{:S(2)}) async-start(), calls=%async_computation | async-start | bytes 16384000 | tf_op jit(solution)/shard_map/all_gather | solution.py:231
  13.4 76.1 %collective-permute-start.1 = (bf16[640,1280]{1,0:T(8,128)(2,1)S(1)}, bf16[640,1280]{1,0:T(8,128)(2,1)S(1)}, u32[]{:S(2)}, u32[]{:S(2)}) collective-permute-start(bf16[640,1280]{1,0:T(8,128)(2,1)S(1)} %copy-done.6), channel_id=1, source_target_pairs={{16,0},{20,4},{24,8},{28,12},{17,1},{21,5},{25,9},{29,13},{18,2},{... | collective-permute-start | bytes 4915208 | tf_op jit(solution)/shard_map/ppermute | solution.py:213
  16.1 60.1 %collective-permute-start.5 = (bf16[1,160,1280]{2,1,0:T(8,128)(2,1)}, bf16[1,160,1280]{2,1,0:T(8,128)(2,1)}, u32[]{:S(2)}, u32[]{:S(2)}) collective-permute-start(bf16[1,160,1280]{2,1,0:T(8,128)(2,1)} %get-tuple-element.47), channel_id=1, source_target_pairs={{0,16},{4,20},{8,24},{12,28},{1,17},{5,21},{9,25},{13,29},{2,18},{... | collective-permute-start | bytes 1228808 | tf_op jit(solution)/shard_map/ppermute | solution.py:220
  30.1 47.9 %collective-permute-start.6 = (bf16[1,160,1280]{2,1,0:T(8,128)(2,1)}, bf16[1,160,1280]{2,1,0:T(8,128)(2,1)S(1)}, u32[]{:S(2)}, u32[]{:S(2)}) collective-permute-start(bf16[1,160,1280]{2,1,0:T(8,128)(2,1)} %get-tuple-element.46), channel_id=1, source_target_pairs={{4,16},{8,20},{12,24},{16,28},{5,17},{9,21},{13,25},{17,29},{6,18}... | collective-permute-start | bytes 1228808 | tf_op jit(solution)/shard_map/ppermute | solution.py:220
  33.3 46.8 %collective-permute-start.7 = (bf16[1,160,1280]{2,1,0:T(8,128)(2,1)}, bf16[1,160,1280]{2,1,0:T(8,128)(2,1)S(1)}, u32[]{:S(2)}, u32[]{:S(2)}) collective-permute-start(bf16[1,160,1280]{2,1,0:T(8,128)(2,1)} %get-tuple-element.45), channel_id=1, source_target_pairs={{8,16},{12,20},{16,24},{20,28},{9,17},{13,21},{17,25},{21,29},{10,... | collective-permute-start | bytes 1228808 | tf_op jit(solution)/shard_map/ppermute | solution.py:220
  36.4 52.3 %collective-permute-start.8 = (bf16[1,160,1280]{2,1,0:T(8,128)(2,1)}, bf16[1,160,1280]{2,1,0:T(8,128)(2,1)S(1)}, u32[]{:S(2)}, u32[]{:S(2)}) collective-permute-start(bf16[1,160,1280]{2,1,0:T(8,128)(2,1)} %get-tuple-element.44), channel_id=1, source_target_pairs={{12,16},{16,20},{20,24},{24,28},{13,17},{17,21},{21,25},{25,29},{1... | collective-permute-start | bytes 1228808 | tf_op jit(solution)/shard_map/ppermute | solution.py:220
  109.7 68.6 %collective-permute-start.19 = (bf16[1,640,640]{2,1,0:T(8,128)(2,1)S(1)}, bf16[1,640,640]{2,1,0:T(8,128)(2,1)}, u32[]{:S(2)}, u32[]{:S(2)}) collective-permute-start(bf16[1,640,640]{2,1,0:T(8,128)(2,1)S(1)} %slice.308), channel_id=1, source_target_pairs={{8,0},{12,4},{16,8},{20,12},{24,16},{28,20},{9,1},{13,5},{17,9},{2... | collective-permute-start | bytes 2457608 | tf_op jit(solution)/shard_map/ppermute | solution.py:240
  117.8 62.4 %collective-permute-start.20 = (bf16[1,640,640]{2,1,0:T(8,128)(2,1)}, bf16[1,640,640]{2,1,0:T(8,128)(2,1)}, u32[]{:S(2)}, u32[]{:S(2)}) collective-permute-start(bf16[1,640,640]{2,1,0:T(8,128)(2,1)} %slice.309), channel_id=1, source_target_pairs={{0,8},{4,12},{8,16},{12,20},{16,24},{20,28},{1,9},{5,13},{9,17},{1... | collective-permute-start | bytes 2457608 | tf_op jit(solution)/shard_map/ppermute | solution.py:241
  121.0 48.2 %collective-permute-start.10 = (bf16[2,640,640]{2,1,0:T(8,128)(2,1)}, bf16[2,640,640]{2,1,0:T(8,128)(2,1)}, u32[]{:S(2)}, u32[]{:S(2)}) collective-permute-start(bf16[2,640,640]{2,1,0:T(8,128)(2,1)} %slice.279), channel_id=1, source_target_pairs={{8,0},{12,4},{16,8},{20,12},{24,16},{28,20},{9,1},{13,5},{17,9},{2... | collective-permute-start | bytes 4915208 | tf_op jit(solution)/shard_map/ppermute | solution.py:240
  127.3 46.2 %collective-permute-start.11 = (bf16[2,640,640]{2,1,0:T(8,128)(2,1)}, bf16[2,640,640]{2,1,0:T(8,128)(2,1)}, u32[]{:S(2)}, u32[]{:S(2)}) collective-permute-start(bf16[2,640,640]{2,1,0:T(8,128)(2,1)} %slice.280), channel_id=1, source_target_pairs={{0,8},{4,12},{8,16},{12,20},{16,24},{20,28},{1,9},{5,13},{9,17},{1... | collective-permute-start | bytes 4915208 | tf_op jit(solution)/shard_map/ppermute | solution.py:241
  129.3 56.8 %collective-permute-start = (s32[10,5,5]{0,2,1:T(8,128)S(1)}, s32[10,5,5]{0,2,1:T(8,128)S(1)}, u32[]{:S(2)}, u32[]{:S(2)}) collective-permute-start(s32[10,5,5]{0,2,1:T(8,128)S(1)} %bitcast.160), channel_id=1, source_target_pairs={{16,0},{20,4},{24,8},{28,12},{17,1},{21,5},{25,9},{29,13},{18,2},{... | collective-permute-start | bytes 3008 | tf_op jit(solution)/shard_map/ppermute | solution.py:301
  169.3 64.5 %collective-permute-start.13 = (bf16[2,640,640]{2,1,0:T(8,128)(2,1)}, bf16[2,640,640]{2,1,0:T(8,128)(2,1)}, u32[]{:S(2)}, u32[]{:S(2)}) collective-permute-start(bf16[2,640,640]{2,1,0:T(8,128)(2,1)} %collective-permute-done.10), channel_id=1, source_target_pairs={{8,0},{12,4},{16,8},{20,12},{9,1},{13,5},{17,9},{21,13},{10,2},{14... | collective-permute-start | bytes 4915208 | tf_op jit(solution)/shard_map/ppermute | solution.py:243
  173.5 60.3 %collective-permute-start.14 = (bf16[2,640,640]{2,1,0:T(8,128)(2,1)}, bf16[2,640,640]{2,1,0:T(8,128)(2,1)}, u32[]{:S(2)}, u32[]{:S(2)}) collective-permute-start(bf16[2,640,640]{2,1,0:T(8,128)(2,1)} %collective-permute-done.11), channel_id=1, source_target_pairs={{8,16},{12,20},{16,24},{20,28},{9,17},{13,21},{17,25},{21,29},{10,... | collective-permute-start | bytes 4915208 | tf_op jit(solution)/shard_map/ppermute | solution.py:244
  178.3 45.6 %collective-permute-start.22 = (bf16[1,640,640]{2,1,0:T(8,128)(2,1)}, bf16[1,640,640]{2,1,0:T(8,128)(2,1)S(1)}, u32[]{:S(2)}, u32[]{:S(2)}) collective-permute-start(bf16[1,640,640]{2,1,0:T(8,128)(2,1)} %collective-permute-done.19), channel_id=1, source_target_pairs={{8,0},{12,4},{16,8},{20,12},{9,1},{13,5},{17,9},{21,13},{10,2},{14... | collective-permute-start | bytes 2457608 | tf_op jit(solution)/shard_map/ppermute | solution.py:243
  180.2 46.2 %collective-permute-start.23 = (bf16[1,640,640]{2,1,0:T(8,128)(2,1)}, bf16[1,640,640]{2,1,0:T(8,128)(2,1)}, u32[]{:S(2)}, u32[]{:S(2)}) collective-permute-start(bf16[1,640,640]{2,1,0:T(8,128)(2,1)} %collective-permute-done.20), channel_id=1, source_target_pairs={{8,16},{12,20},{16,24},{20,28},{9,17},{13,21},{17,25},{21,29},{10,... | collective-permute-start | bytes 2457608 | tf_op jit(solution)/shard_map/ppermute | solution.py:244
  228.1 58.1 %collective-permute-start.25 = (bf16[1,640,640]{2,1,0:T(8,128)(2,1)}, bf16[1,640,640]{2,1,0:T(8,128)(2,1)}, u32[]{:S(2)}, u32[]{:S(2)}) collective-permute-start(bf16[1,640,640]{2,1,0:T(8,128)(2,1)} %get-tuple-element.12), channel_id=1, source_target_pairs={{0,8},{4,12},{16,24},{20,28},{8,0},{12,4},{24,16},{28,20},{1,9},{5... | collective-permute-start | bytes 2457608 | tf_op jit(solution)/shard_map/ppermute | solution.py:246
  237.9 68.0 %collective-permute-start.9 = (bf16[2,640,640]{2,1,0:T(8,128)(2,1)}, bf16[2,640,640]{2,1,0:T(8,128)(2,1)}, u32[]{:S(2)}, u32[]{:S(2)}) collective-permute-start(bf16[2,640,640]{2,1,0:T(8,128)(2,1)} %get-tuple-element.17), channel_id=1, source_target_pairs={{0,4},{4,0},{8,12},{12,8},{16,20},{20,16},{24,28},{28,24},{1,5},{5... | collective-permute-start | bytes 4915208 | tf_op jit(solution)/shard_map/ppermute | solution.py:252
  237.9 103.1 %collective-permute-start.15 = (bf16[2,640,640]{2,1,0:T(8,128)(2,1)}, bf16[2,640,640]{2,1,0:T(8,128)(2,1)}, u32[]{:S(2)}, u32[]{:S(2)}) collective-permute-start(bf16[2,640,640]{2,1,0:T(8,128)(2,1)} %get-tuple-element.16), channel_id=1, source_target_pairs={{0,4},{4,0},{8,12},{12,8},{16,20},{20,16},{24,28},{28,24},{1,5},{5... | collective-permute-start | bytes 4915208 | tf_op jit(solution)/shard_map/ppermute | solution.py:252
  270.8 247.5 %collective-permute-start.21 = (bf16[1,640,640]{2,1,0:T(8,128)(2,1)}, bf16[1,640,640]{2,1,0:T(8,128)(2,1)}, u32[]{:S(2)}, u32[]{:S(2)}) collective-permute-start(bf16[1,640,640]{2,1,0:T(8,128)(2,1)} %broadcast_select_fusion.6), channel_id=1, source_target_pairs={{0,4},{4,0},{8,12},{12,8},{16,20},{20,16},{24,28},{28,24},{1,5},{5... | collective-permute-start | bytes 2457608 | tf_op jit(solution)/shard_map/ppermute | solution.py:252
  279.7 241.4 %collective-permute-start.18 = (bf16[1,640,640]{2,1,0:T(8,128)(2,1)}, bf16[1,640,640]{2,1,0:T(8,128)(2,1)}, u32[]{:S(2)}, u32[]{:S(2)}) collective-permute-start(bf16[1,640,640]{2,1,0:T(8,128)(2,1)} %get-tuple-element.14), channel_id=1, source_target_pairs={{0,4},{4,0},{8,12},{12,8},{16,20},{20,16},{24,28},{28,24},{1,5},{5... | collective-permute-start | bytes 2457608 | tf_op jit(solution)/shard_map/ppermute | solution.py:252
  286.1 246.1 %collective-permute-start.24 = (bf16[1,640,640]{2,1,0:T(8,128)(2,1)}, bf16[1,640,640]{2,1,0:T(8,128)(2,1)}, u32[]{:S(2)}, u32[]{:S(2)}) collective-permute-start(bf16[1,640,640]{2,1,0:T(8,128)(2,1)} %get-tuple-element.13), channel_id=1, source_target_pairs={{0,4},{4,0},{8,12},{12,8},{16,20},{20,16},{24,28},{28,24},{1,5},{5... | collective-permute-start | bytes 2457608 | tf_op jit(solution)/shard_map/ppermute | solution.py:252
  305.9 233.4 %collective-permute-start.26 = (bf16[1,640,640]{2,1,0:T(8,128)(2,1)}, bf16[1,640,640]{2,1,0:T(8,128)(2,1)}, u32[]{:S(2)}, u32[]{:S(2)}) collective-permute-start(bf16[1,640,640]{2,1,0:T(8,128)(2,1)} %collective-permute-done.25), channel_id=1, source_target_pairs={{0,4},{4,0},{8,12},{12,8},{16,20},{20,16},{24,28},{28,24},{1,5},{5... | collective-permute-start | bytes 2457608 | tf_op jit(solution)/shard_map/ppermute | solution.py:252
  341.0 101.3 %collective-permute-start.17 = (bf16[2,640,640]{2,1,0:T(8,128)(2,1)}, bf16[2,640,640]{2,1,0:T(8,128)(2,1)S(1)}, u32[]{:S(2)}, u32[]{:S(2)}) collective-permute-start(bf16[2,640,640]{2,1,0:T(8,128)(2,1)} %collective-permute-done.16), channel_id=1, source_target_pairs={{0,4},{4,0},{8,12},{12,8},{16,20},{20,16},{24,28},{28,24},{1,5},{5... | collective-permute-start | bytes 4915208 | tf_op jit(solution)/shard_map/ppermute | solution.py:252
  566.8 44.6 %collective-permute-start.27 = (bf16[4,160,640]{2,1,0:T(8,128)(2,1)S(1)}, bf16[4,160,640]{2,1,0:T(8,128)(2,1)}, u32[]{:S(2)}, u32[]{:S(2)}) collective-permute-start(bf16[4,160,640]{2,1,0:T(8,128)(2,1)S(1)} %slice.311), channel_id=1, source_target_pairs={{0,16},{4,20},{8,24},{12,28},{1,17},{5,21},{9,25},{13,29},{2,18},{... | collective-permute-start | bytes 2457608 | tf_op jit(solution)/shard_map/ppermute | solution.py:307
  (32 other events, 753.7 us)
Sparse Core Ops, SparseCore 0:
  92.8 88.7 all-gather.1

commit v2 on v1

--- a/solution.py
+++ b/solution.py
@@ -183,15 +183,250 @@
     )(role, bias, queries, keys_n, values)
 
 
+def spread_kernel(
+    x_ref, own_ref, oth_ref, xg_ref, wg_ref, relay_ref,
+    x_send, x_recv, near_send, near_recv, core_send, core_recv, pass_send, pass_recv,
+    mate_send, mate_recv, cross_send, relay_recv, fwd_send, a1_send, a1_recv, a2_send, a2_recv,
+    y_send, y_recv, local_sem,
+):
+    me, fs = lax.axis_index("seq"), lax.axis_index("fsdp")
+    quarter, feats = x_ref.shape[1:]
+    kinds = own_ref.shape[0]
+    half = 4
+    z, y = me // 2, me % 2
+    mate = (z + 1 - 2 * (z % 2)) * 2 + y
+    side = z // 2
+    a1 = (2 - side) * 2 + y
+    a2 = (3 - 3 * side) * 2 + y
+    other_y = z * 2 + 1 - y
+    inner = (z == 1) | (z == 2)
+    outer = (z == 0) | (z == 3)
+    is_spatial = me < half
+    is_temporal = me >= half
+    sib = fs + 1 - 2 * (fs % 2)
+    across = (fs + 2) % 4
+
+    barrier = pltpu.get_barrier_semaphore()
+    for r in range(1, 8):
+        pl.semaphore_signal(
+            barrier, inc=1, device_id=((me + r) % 8, fs), device_id_type=pl.DeviceIdType.MESH
+        )
+    for f in (sib, across):
+        pl.semaphore_signal(barrier, inc=1, device_id=(me, f), device_id_type=pl.DeviceIdType.MESH)
+    pl.semaphore_wait(barrier, 9)
+
+    def remote(src, dst, send, recv, seq, fsdp):
+        return pltpu.make_async_remote_copy(
+            src_ref=src, dst_ref=dst, send_sem=send, recv_sem=recv,
+            device_id=(seq, fsdp), device_id_type=pl.DeviceIdType.MESH,
+        )
+
+    def x_cols(f):
+        return pl.ds(pl.multiple_of(f * feats, 128), feats)
+
+    def slot(r, f):
+        return xg_ref.at[r, :, x_cols(f)]
+
+    def to_temporal(j):
+        target = half + j
+        r = (me + 8 - target) % 8
+        return remote(x_ref.at[j], slot(r, fs), x_send.at[j], x_recv.at[r], target, fs)
+
+    def to_spatial(j):
+        target = (me + half) % 8
+        return remote(
+            x_ref.at[j], slot(half + j, fs), x_send.at[half + j], x_recv.at[half + j], target, fs
+        )
+
+    def keep_spatial(j):
+        return pltpu.make_async_copy(x_ref.at[j], slot(j, fs), local_sem.at[kinds + j])
+
+    def keep_temporal():
+        return pltpu.make_async_copy(x_ref.at[me % half], slot(0, fs), local_sem.at[kinds])
+
+    for j in range(half):
+        @pl.when(me != half + j)
+        def _():
+            to_temporal(j).start()
+
+        @pl.when(is_temporal)
+        def _():
+            to_spatial(j).start()
+
+        @pl.when(is_spatial)
+        def _():
+            keep_spatial(j).start()
+
+    @pl.when(is_temporal)
+    def _():
+        keep_temporal().start()
+
+    def mate_copy(i):
+        return remote(own_ref.at[i], wg_ref.at[i, me], mate_send.at[i], mate_recv.at[i], mate, fs)
+
+    def relay_copy(i):
+        return remote(oth_ref.at[i], relay_ref.at[i], cross_send.at[i], relay_recv.at[i], mate, fs)
+
+    def cross_copy(i):
+        return remote(oth_ref.at[i], wg_ref.at[i, me], cross_send.at[i], a1_recv.at[i], a1, fs)
+
+    def fwd_copy(i):
+        return remote(relay_ref.at[i], wg_ref.at[i, mate], fwd_send.at[i], a2_recv.at[i], a1, fs)
+
+    def a1_copy(i):
+        at = wg_ref.at[i, a1]
+        return remote(at, at, a1_send.at[i], a1_recv.at[i], mate, fs)
+
+    def a2_copy(i):
+        at = wg_ref.at[i, a2]
+        return remote(at, at, a2_send.at[i], a2_recv.at[i], mate, fs)
+
+    def y_copy(i, k):
+        row = (me, mate, a1, a2)[k]
+        src = own_ref.at[i] if k == 0 else wg_ref.at[i, row]
+        return remote(src, wg_ref.at[i, row], y_send.at[i, k], y_recv.at[i, k], other_y, fs)
+
+    def keep_w(i):
+        return pltpu.make_async_copy(own_ref.at[i], wg_ref.at[i, me], local_sem.at[i])
+
+    for i in range(kinds):
+        mate_copy(i).start()
+
+        @pl.when(outer)
+        def _():
+            relay_copy(i).start()
+
+        @pl.when(inner)
+        def _():
+            cross_copy(i).start()
+
+        y_copy(i, 0).start()
+        keep_w(i).start()
+
+    def near_copy(r):
+        return remote(slot(r, fs), slot(r, fs), near_send.at[r], near_recv.at[r], me, across)
+
+    def core_copy(r):
+        return remote(slot(r, fs), slot(r, fs), core_send.at[r], core_recv.at[r], me, sib)
+
+    def pass_copy(r):
+        at = slot(r, across)
+        return remote(at, at, pass_send.at[r], pass_recv.at[r], me, sib)
+
+    def x_arrived(r):
+        remote(x_ref.at[0], slot(r, fs), x_send.at[0], x_recv.at[r], me, across).wait_recv()
+
+    for r in range(8):
+        if r == 0:
+            @pl.when(is_temporal)
+            def _():
+                keep_temporal().wait()
+        else:
+            @pl.when(is_temporal)
+            def _():
+                x_arrived(r)
+        if r < half:
+            @pl.when(is_spatial)
+            def _():
+                keep_spatial(r).wait()
+        else:
+            @pl.when(is_spatial)
+            def _():
+                x_arrived(r)
+        near_copy(r).start()
+        core_copy(r).start()
+
+    for i in range(kinds):
+        mate_copy(i).wait_recv()
+        y_copy(i, 1).start()
+
+        @pl.when(inner)
+        def _():
+            relay_copy(i).wait_recv()
+            fwd_copy(i).start()
+
+        a1_copy(i).wait_recv()
+
+        @pl.when(inner)
+        def _():
+            a1_copy(i).start()
+
+        y_copy(i, 2).start()
+
+    for r in range(8):
+        remote(
+            slot(r, across), slot(r, across), near_send.at[r], near_recv.at[r], me, across
+        ).wait_recv()
+        pass_copy(r).start()
+
+    for i in range(kinds):
+        a2_copy(i).wait_recv()
+
+        @pl.when(inner)
+        def _():
+            a2_copy(i).start()
+
+        y_copy(i, 3).start()
+
+    for r in range(8):
+        core_copy(r).wait_recv()
+        pass_copy(r).wait_recv()
+        near_copy(r).wait_send()
+        core_copy(r).wait_send()
+        pass_copy(r).wait_send()
+    for j in range(half):
+        @pl.when(me != half + j)
+        def _():
+            to_temporal(j).wait_send()
+
+        @pl.when(is_temporal)
+        def _():
+            to_spatial(j).wait_send()
+
+    for i in range(kinds):
+        keep_w(i).wait()
+        mate_copy(i).wait_send()
+        cross_copy(i).wait_send()
+
+        @pl.when(inner)
+        def _():
+            fwd_copy(i).wait_send()
+            a1_copy(i).wait_send()
+            a2_copy(i).wait_send()
+
+        for k in range(4):
+            y_copy(i, k).wait()
+
+
+def spread(x_quarters, w_own, w_oth, seq_count, fsdp_count):
+    half, quarter, feats = x_quarters.shape
+    kinds, rows, cols = w_own.shape
+    dma = pltpu.SemaphoreType.DMA
+    any_spec = pl.BlockSpec(memory_space=pl.ANY)
+    sent = jnp.bfloat16
+    return pl.pallas_call(
+        spread_kernel,
+        out_shape=[
+            jax.ShapeDtypeStruct((seq_count, quarter, feats * fsdp_count), sent),
+            jax.ShapeDtypeStruct((kinds, seq_count, rows, cols), sent),
+            jax.ShapeDtypeStruct((kinds, rows, cols), sent),
+        ],
+        in_specs=[any_spec] * 3,
+        out_specs=[any_spec] * 3,
+        scratch_shapes=[dma((8,))] * 8
+        + [dma((kinds,))] * 9
+        + [dma((kinds, 4)), dma((kinds, 4)), dma((kinds + half,))],
+        compiler_params=pltpu.CompilerParams(
+            collective_id=0, has_side_effects=True, vmem_limit_bytes=32 * 1024 * 1024
+        ),
+    )(x_quarters, w_own, w_oth)
+
+
 def pick_heads(array, heads):
     return jnp.concatenate(
         [lax.dynamic_slice_in_dim(array, head * HD, HD, axis=array.ndim - 1) for head in heads],
         axis=-1,
     )
-
-
-def along_z(shift, froms):
-    return [(2 * z + y, 2 * (z + shift) + y) for z in froms for y in range(2)]
 
 
 def split_shards(x_tokens, w_qkv, q_gain, k_gain, head_kind, block_live):
@@ -209,79 +444,36 @@
     tm_heads = [order[kept + i] for i in range(kept)]
     my_heads = [jnp.where(is_spatial, s, t) for s, t in zip(sp_heads, tm_heads)]
 
-    up_half = [(i + half, i) for i in range(half)]
-    second = lax.ppermute(x_tokens, "seq", up_half)
-    grid = x_tokens.reshape(half, quarter, feats)
-    parts = [lax.dynamic_index_in_dim(grid, jnp.maximum(me - half, 0), 0)]
-    for r in range(1, seq_count):
-        target = (me - r) % seq_count
-        block = lax.dynamic_index_in_dim(grid, jnp.maximum(target - half, 0), 0)
-        parts.append(
-            lax.ppermute(
-                block, "seq", [((d + r) % seq_count, d) for d in range(half, seq_count)]
-            )
-        )
-    mine = jnp.where(
-        is_spatial,
-        jnp.concatenate([grid, second.reshape(grid.shape)], axis=0),
-        jnp.concatenate(parts, axis=0),
-    ).reshape(2 * rows, feats)
-    hf = feats // 2
-    mine = jnp.where(y == 0, mine, jnp.concatenate([mine[:, hf:], mine[:, :hf]], axis=1))
-    feats_of = lax.all_gather(mine, "fsdp", axis=0, tiled=False)
-
-    w_sp, w_tm = pick_heads(w_qkv, sp_heads), pick_heads(w_qkv, tm_heads)
-    swap_y = [(i, i ^ 1) for i in range(seq_count)]
-    turn = jnp.where(is_spatial, 1, -1)
-    at_z = [z, z + turn, z + 2 * turn, jnp.where(z % 2 == 0, 3, 0)]
-
-    def gather_rows(sp, tm):
-        own = jnp.where(is_spatial, sp, tm)
-        down = lax.ppermute(sp, "seq", along_z(-1, (1, 2, 3)))
-        up = lax.ppermute(tm, "seq", along_z(1, (0, 1, 2)))
-        near = jnp.where(is_spatial, down, up)
-        down2 = lax.ppermute(down, "seq", along_z(-1, (1, 2)))
-        up2 = lax.ppermute(up, "seq", along_z(1, (1, 2)))
-        far = jnp.where(is_spatial, down2, up2)
-        last = lax.ppermute(
-            jnp.where((z == 0) | (z == 3), own, far),
-            "seq",
-            along_z(1, (0, 2)) + along_z(-1, (1, 3)),
-        )
-        held = [own, near, far, last]
-        return [(piece, lax.ppermute(piece, "seq", swap_y)) for piece in held]
-
-    def project(pieces, count):
-        totals = [None] * count
-        for z_at, (own, other) in zip(at_z, pieces):
-            feat = lax.dynamic_index_in_dim(feats_of, z_at, 0, keepdims=False)
-            for part, rows_w in ((feat[:, :hf], own), (feat[:, hf:], other)):
-                for i in range(count):
-                    term = jnp.dot(part, rows_w[i], preferred_element_type=jnp.float32)
-                    totals[i] = term if totals[i] is None else totals[i] + term
-        return totals
-
-    q_raw, k_raw = project(gather_rows(w_sp[:2], w_tm[:2]), 2)
-    (v_raw,) = project(gather_rows(w_sp[2:], w_tm[2:]), 1)
+    other_heads = [jnp.where(is_spatial, t, s) for s, t in zip(sp_heads, tm_heads)]
+
+    tokens, weights, _ = spread(
+        x_tokens.reshape(half, quarter, feats),
+        pick_heads(w_qkv, my_heads),
+        pick_heads(w_qkv, other_heads),
+        seq_count,
+        lax.axis_size("fsdp"),
+    )
+    tokens = tokens.reshape(2 * rows, -1)
+    weights = weights.reshape(weights.shape[0], -1, kept * HD)
+    q_raw, k_raw, v_raw = [
+        jnp.dot(tokens, weights[i], preferred_element_type=jnp.float32) for i in range(3)
+    ]
 
     sq = jnp.stack([jnp.sum(q_raw * q_raw, axis=1), jnp.sum(k_raw * k_raw, axis=1)])
-    blank = jnp.zeros((2, seq_count, rows), jnp.float32)
-    sq_sp = sq.reshape(2, 2, rows)
-    of_sp = lax.dynamic_update_slice(blank, sq_sp[:, :1], (0, me % half, 0))
-    of_sp = lax.dynamic_update_slice(of_sp, sq_sp[:, 1:], (0, me % half + half, 0))
-    frame_at = (jnp.arange(seq_count) - me) % seq_count
+    sums = lax.all_gather(lax.psum(sq, "fsdp"), "seq", axis=0, tiled=False)
+    of_sp = sums[:half].reshape(half, 2, 2, rows).transpose(1, 2, 0, 3)
+    of_sp = of_sp.reshape(2, seq_count, rows)
+    of_tm = sums[half:].reshape(half, 2, seq_count, quarter).transpose(1, 2, 0, 3)
+    of_tm = jnp.stack(
+        [
+            jnp.take(of_tm[:, :, q], (jnp.arange(seq_count) - half - q) % seq_count, axis=1)
+            for q in range(half)
+        ],
+        axis=2,
+    ).reshape(2, seq_count, rows)
+    sums = of_sp + of_tm
+    sums_sp = jnp.take(sums, me % half + jnp.arange(2) * half, axis=1).reshape(2, 2 * rows)
     pos_at = jnp.maximum(me - half, 0) * quarter
-    of_tm = lax.dynamic_update_slice(
-        blank, jnp.take(sq.reshape(2, seq_count, quarter), frame_at, axis=1), (0, 0, pos_at)
-    )
-    sums = lax.psum(jnp.where(is_spatial, of_sp, of_tm), ("seq", "fsdp"))
-    sums_sp = jnp.concatenate(
-        [
-            lax.dynamic_slice(sums, (0, me % half, 0), (2, 1, rows)),
-            lax.dynamic_slice(sums, (0, me % half + half, 0), (2, 1, rows)),
-        ],
-        axis=1,
-    ).reshape(2, 2 * rows)
     slot_at = (jnp.arange(seq_count) + me) % seq_count
     sums_tm = jnp.take(
         lax.dynamic_slice(sums, (0, 0, pos_at), (2, seq_count, quarter)), slot_at, axis=1
@@ -297,6 +489,7 @@
     keys_n = normed(k_raw, my_sums[1], k_gain)
     values = v_raw.astype(jnp.bfloat16).reshape(seq_count, quarter, kept * HD)
 
+    up_half = [(i + half, i) for i in range(half)]
     live = block_live[0]
     live_two = jnp.stack([live, lax.ppermute(live, "seq", up_half)])
     live_two = jnp.take(live_two, order[:kept], axis=1)

time: 631 us -> 480 us (0.76); the launches traced: 621 us -> 479 us
  Pallas kernels: 22.2 us -> 257 us
  waiting for transfers between devices: 249 us -> 19.3 us
  starting transfers between devices: 124 us -> 19.3 us
  matrix products: 72.2 us -> 37.8 us
  blocking collectives: 45.8 us -> 72.1 us
  between operations: 33.9 us -> 19.3 us
  local copies, waits for them, and re-layouts: 54.9 us -> 44.2 us
  other arithmetic: 19.5 us -> 9.94 us
    pallas_call x0 -> x1, Pallas kernels: none -> 235 us  [spread(): pl.pallas_call(spread_kernel, out_shape=[jax.ShapeDtypeStruct((seq_count,...]
    ppermute x26 -> x0, waiting for transfers between devices: 226 us -> none  [the longest x8 156 us: gather_rows(): return [(piece, lax.ppermute(piece, 'seq', swap_y)) for piece in held]]
    ppermute x26 -> x0, starting transfers between devices: 107 us -> none  [the longest x7 58.9 us: split_shards(): lax.ppermute(block, 'seq', [((d + r) % seq_count, d) for d in range(half,...]
    all_gather x0 -> x1, blocking collectives: none -> 61.9 us  [split_shards(): sums = lax.all_gather(lax.psum(sq, 'fsdp'), 'seq', axis=0, tiled=False)]
    psum x1, blocking collectives: 45.8 us -> 10.1 us  [split_shards(): sums = lax.all_gather(lax.psum(sq, 'fsdp'), 'seq', axis=0, tiled=False)]
    dot_general x24 -> x3, matrix products: 72.2 us -> 37.8 us  [split_shards(): jnp.dot(tokens, weights[i], preferred_element_type=jnp.float32)]
    select_n x9 -> x3, other arithmetic: 13.8 us -> 0.03 us  [the longest x2 0.02 us: split_shards(): jnp.take(of_tm[:, :, q], (jnp.arange(seq_count) - half - q) % seq_count,...]
    unnamed x65 -> x29, local copies, waits for them, and re-layouts: 29.7 us -> 21.4 us
  transfers between devices with their start and end apart: 36 -> 9, of which waited for: 15 -> 4; matrix products, arithmetic and copies ran while one was open for 21% -> 17% of each run, Pallas kernels for 0% -> 49%
where the time goes in v2:
time: 480 us; the launch traced here: 479 us
  Pallas kernels  257 us (54%)
  blocking collectives  72.1 us (15%)
  local copies, waits for them, and re-layouts  44.2 us (9%)
  matrix products  37.8 us (8%)
  starting transfers between devices  19.3 us (4%)
  waiting for transfers between devices  19.3 us (4%)
  between operations  19.3 us (4%)
  other arithmetic  9.94 us (2%)
    pallas_call x1, Pallas kernels, spread(): pl.pallas_call(spread_kernel, out_shape=[jax.ShapeDtypeStruct((seq_count,...  235 us
    all_gather x1, blocking collectives, split_shards(): sums = lax.all_gather(lax.psum(sq, 'fsdp'), 'seq', axis=0, tiled=False)  61.9 us
    dot_general x3, matrix products, split_shards(): jnp.dot(tokens, weights[i], preferred_element_type=jnp.float32)  37.8 us
    pallas_call x1, Pallas kernels, attend(): pl.pallas_call(attend_kernel, grid=(cols // HD,), out_shape=jax.ShapeDtyp...  22.2 us
    unnamed x29, local copies, waits for them, and re-layouts  21.4 us
    ppermute x7, waiting for transfers between devices, split_shards(): lax.ppermute(done[r:r + 1], 'seq', [(s, (s + r) % seq_count) for s in ran...  19.3 us
    ppermute x1, starting transfers between devices, split_shards(): lax.ppermute(done[half:], 'seq', [(i, i + half) for i in range(half)])  10.9 us
    psum x1, blocking collectives, split_shards(): sums = lax.all_gather(lax.psum(sq, 'fsdp'), 'seq', axis=0, tiled=False)  10.1 us
  transfers between devices with their start and end apart: 9, of which 4 were waited for; matrix products, arithmetic and copies ran while one was open for 17% of the time, Pallas kernels for 49%

profile of v2, /device:TPU:12, one launch (start us, length us, event | category | flops | bytes accessed | tf_op | source)
XLA Modules:
  0.0 479.2 jit_solution(15500771491227901729)
XLA Ops:
  2.0 1.9 sort.34
  25.1 1.4 dynamic-slice_dynamic-update-slice_fusion.4
  26.5 1.4 dynamic-slice_dynamic-update-slice_fusion.3
  27.9 1.4 dynamic-slice_dynamic-update-slice_fusion.2
  29.4 1.6 dynamic-slice_dynamic-update-slice_fusion.1
  30.9 1.4 dynamic-slice_dynamic-update-slice_fusion
  32.4 235.2 %shard_map.64 = (bf16[8,160,5120]{2,1,0:T(8,128)(2,1)S(1)}, bf16[3,8,640,640]{3,2,1,0:T(8,128)(2,1)}, bf16[3,640,640]{2,1,0:T(8,128)(2,1)}) custom-call(bf16[4,160,1280]{2,1,0:T(8,128)(2,1)S(1)} %bitcast.88, bf16[3,640,640]{2,1,0:T(8,128)(2,1)S(1)} %get-tuple-element.22.own_ref, bf16[3,640,640]{2,1,0:T(8,128)(2,1)S(1)} %get-tuple-element.21.oth_ref), custom_call_target="tpu_custom_call" | custom-call | tf_op jit(solution)/shard_map/pallas_call | solution.py:407
  267.5 9.7 %fusion.36 = (bf16[1,8,640,640]{3,2,1,0:T(8,128)(2,1)}, bf16[1,8,640,640]{3,2,1,0:T(8,128)(2,1)S(1)}, bf16[1,8,640,640]{3,2,1,0:T(8,128)(2,1)S(1)}) fusion(bf16[3,8,640,640]{3,2,1,0:T(8,128)(2,1)} %get-tuple-element.12), kind=kLoop, calls=%fused_computation.166 | loop fusion | bytes 39321600 | tf_op jit(solution)/shard_map/slice | solution.py:459
  277.2 13.3 %convolution_convert_fusion = bf16[1280,640]{1,0:T(8,128)(2,1)} fusion(bf16[1280,5120]{1,0:T(8,128)(2,1)S(1)} %bitcast.90, bf16[5120,640]{1,0:T(8,128)(2,1)} %bitcast.105), kind=kOutput, calls=%fused_computation.32 | convolution fusion | flops 8389427200 | bytes 21299200 | tf_op jit(solution)/shard_map/dot_general | solution.py:459
  290.5 12.1 %multiply_reduce_fusion = (f32[1280]{0:T(1024)S(1)}, f32[1280,640]{1,0:T(8,128)}) fusion(bf16[1280,5120]{1,0:T(8,128)(2,1)S(1)} %bitcast.91, bf16[5120,640]{1,0:T(8,128)(2,1)S(1)} %bitcast.104), kind=kOutput, calls=%fused_computation.30 | convolution fusion | flops 8390245376 | bytes 22942720 | tf_op jit(solution)/shard_map/dot_general | solution.py:459
  302.7 12.3 %multiply_reduce_fusion.1 = (f32[1280]{0:T(1024)S(1)}, f32[1280,640]{1,0:T(8,128)}) fusion(bf16[1280,5120]{1,0:T(8,128)(2,1)S(1)} %bitcast.92, bf16[5120,640]{1,0:T(8,128)(2,1)S(1)} %bitcast.103), kind=kOutput, calls=%fused_computation.31 | convolution fusion | flops 8390245376 | bytes 22942720 | tf_op jit(solution)/shard_map/dot_general | solution.py:459
  315.0 10.1 %psum.7 = f32[1,2,1280]{2,1,0:T(2,128)S(1)} all-reduce(f32[1,2,1280]{2,1,0:T(2,128)S(1)} %maximum_bitcast_fusion), channel_id=1, replica_groups=mesh['seq'=8,'fsdp'=4] {'fsdp'}, use_global_device_ids=true, to_apply=%region_3.4 | all-reduce | flops 2560 | bytes 20480 | tf_op jit(solution)/shard_map/psum | solution.py:463
  325.1 61.9 %all_gather.7 = f32[8,2,1280]{2,1,0:T(2,128)S(1)} all-gather(f32[1,2,1280]{2,1,0:T(2,128)S(1)} %psum.7), channel_id=1, replica_groups=mesh['seq'=8,'fsdp'=4] {'seq'}, dimensions={0}, use_global_device_ids=true | all-gather | bytes 92160 | tf_op jit(solution)/shard_map/all_gather | solution.py:463
  399.4 2.4 multiply_convert_fusion
  402.3 1.5 multiply_convert_fusion.1
  405.5 1.4 copy-done
  407.0 1.4 copy-done.2
  408.4 22.2 %shard_map.65 = bf16[8,160,640]{2,1,0:T(8,128)(2,1)S(1)} custom-call(s32[1]{0:T(128)} %bitcast.role_ref, f32[2,5,25]{2,1,0:T(8,128)S(1)} %fusion.20.bias_ref, bf16[8,160,640]{2,1,0:T(8,128)(2,1)S(1)} %bitcast.87, bf16[8,160,640]{2,1,0:T(8,128)(2,1)S(1)} %bitcast.86, bf16[8,160,640]{2,1,0:T(8,128)(2,1)S(1)} %bitcast.89), custom_call_target="tpu_custom_call" | custom-call | tf_op jit(solution)/shard_map/pallas_call | solution.py:170
  432.9 10.9 %collective-permute-start.1 = (bf16[4,160,640]{2,1,0:T(8,128)(2,1)S(1)}, bf16[4,160,640]{2,1,0:T(8,128)(2,1)}, u32[]{:S(2)}, u32[]{:S(2)}) collective-permute-start(bf16[4,160,640]{2,1,0:T(8,128)(2,1)S(1)} %slice.196), channel_id=1, source_target_pairs={{0,16},{4,20},{8,24},{12,28},{1,17},{5,21},{9,25},{13,29},{2,18},{... | collective-permute-start | bytes 2457608 | tf_op jit(solution)/shard_map/ppermute | solution.py:500
  451.7 6.3 %collective-permute-done.5 = bf16[1,160,640]{2,1,0:T(8,128)(2,1)S(1)} collective-permute-done((bf16[1,160,640]{2,1,0:T(8,128)(2,1)S(1)}, bf16[1,160,640]{2,1,0:T(8,128)(2,1)S(1)}, u32[]{:S(2)}, u32[]{:S(2)}) %collective-permute-start.5) | collective-permute-done | bytes 204832 | tf_op jit(solution)/shard_map/ppermute | solution.py:505
  458.7 2.9 collective-permute-done.6
  462.3 6.6 %collective-permute-done.7 = bf16[1,160,640]{2,1,0:T(8,128)(2,1)S(1)} collective-permute-done((bf16[1,160,640]{2,1,0:T(8,128)(2,1)S(1)}, bf16[1,160,640]{2,1,0:T(8,128)(2,1)S(1)}, u32[]{:S(2)}, u32[]{:S(2)}) %collective-permute-start.7) | collective-permute-done | bytes 204832 | tf_op jit(solution)/shard_map/ppermute | solution.py:505
  469.7 3.5 collective-permute-done.8
  473.9 2.1 gather_fusion.2
  (117 shorter events, 34.8 us)
Async XLA Ops:
  0.7 403.9 %collective-permute-start = (s32[10,5,5]{0,2,1:T(8,128)S(1)}, s32[10,5,5]{0,2,1:T(8,128)S(1)}, u32[]{:S(2)}, u32[]{:S(2)}) collective-permute-start(s32[10,5,5]{0,2,1:T(8,128)S(1)} %bitcast.111), channel_id=1, source_target_pairs={{16,0},{20,4},{24,8},{28,12},{17,1},{21,5},{25,9},{29,13},{18,2},{... | collective-permute-start | bytes 3008 | tf_op jit(solution)/shard_map/ppermute | solution.py:494
  29.4 3.0 copy-start.1
  399.4 2.9 copy-start.3
  405.5 1.4 copy-start
  407.0 1.4 copy-start.2
  431.4 14.3 %collective-permute-start.2 = (bf16[1,160,640]{2,1,0:T(8,128)(2,1)S(1)}, bf16[1,160,640]{2,1,0:T(8,128)(2,1)S(1)}, u32[]{:S(2)}, u32[]{:S(2)}) collective-permute-start(bf16[1,160,640]{2,1,0:T(8,128)(2,1)S(1)} %get-tuple-element.37), channel_id=1, source_target_pairs={{16,20},{20,24},{24,28},{28,0},{17,21},{21,25},{25,29},{29,1},{18,... | collective-permute-start | bytes 614408 | tf_op jit(solution)/shard_map/ppermute | solution.py:505
  432.1 15.7 %collective-permute-start.3 = (bf16[1,160,640]{2,1,0:T(8,128)(2,1)S(1)}, bf16[1,160,640]{2,1,0:T(8,128)(2,1)S(1)}, u32[]{:S(2)}, u32[]{:S(2)}) collective-permute-start(bf16[1,160,640]{2,1,0:T(8,128)(2,1)S(1)} %get-tuple-element.36), channel_id=1, source_target_pairs={{16,24},{20,28},{24,0},{28,4},{17,25},{21,29},{25,1},{29,5},{18,26... | collective-permute-start | bytes 614408 | tf_op jit(solution)/shard_map/ppermute | solution.py:505
  432.9 43.3 %collective-permute-start.1 = (bf16[4,160,640]{2,1,0:T(8,128)(2,1)S(1)}, bf16[4,160,640]{2,1,0:T(8,128)(2,1)}, u32[]{:S(2)}, u32[]{:S(2)}) collective-permute-start(bf16[4,160,640]{2,1,0:T(8,128)(2,1)S(1)} %slice.196), channel_id=1, source_target_pairs={{0,16},{4,20},{8,24},{12,28},{1,17},{5,21},{9,25},{13,29},{2,18},{... | collective-permute-start | bytes 2457608 | tf_op jit(solution)/shard_map/ppermute | solution.py:500
  443.8 6.0 %collective-permute-start.4 = (bf16[1,160,640]{2,1,0:T(8,128)(2,1)S(1)}, bf16[1,160,640]{2,1,0:T(8,128)(2,1)S(1)}, u32[]{:S(2)}, u32[]{:S(2)}) collective-permute-start(bf16[1,160,640]{2,1,0:T(8,128)(2,1)S(1)} %get-tuple-element.35), channel_id=1, source_target_pairs={{16,28},{20,0},{24,4},{28,8},{17,29},{21,1},{25,5},{29,9},{18,30},... | collective-permute-start | bytes 614408 | tf_op jit(solution)/shard_map/ppermute | solution.py:505
  444.4 13.6 %collective-permute-start.5 = (bf16[1,160,640]{2,1,0:T(8,128)(2,1)S(1)}, bf16[1,160,640]{2,1,0:T(8,128)(2,1)S(1)}, u32[]{:S(2)}, u32[]{:S(2)}) collective-permute-start(bf16[1,160,640]{2,1,0:T(8,128)(2,1)S(1)} %get-tuple-element.34), channel_id=1, source_target_pairs={{16,0},{20,4},{24,8},{28,12},{17,1},{21,5},{25,9},{29,13},{18,2},{... | collective-permute-start | bytes 614408 | tf_op jit(solution)/shard_map/ppermute | solution.py:505
  445.8 15.9 %collective-permute-start.6 = (bf16[1,160,640]{2,1,0:T(8,128)(2,1)S(1)}, bf16[1,160,640]{2,1,0:T(8,128)(2,1)S(1)}, u32[]{:S(2)}, u32[]{:S(2)}) collective-permute-start(bf16[1,160,640]{2,1,0:T(8,128)(2,1)S(1)} %get-tuple-element.33), channel_id=1, source_target_pairs={{16,4},{20,8},{24,12},{28,16},{17,5},{21,9},{25,13},{29,17},{18,6}... | collective-permute-start | bytes 614408 | tf_op jit(solution)/shard_map/ppermute | solution.py:505
  447.8 21.2 %collective-permute-start.7 = (bf16[1,160,640]{2,1,0:T(8,128)(2,1)S(1)}, bf16[1,160,640]{2,1,0:T(8,128)(2,1)S(1)}, u32[]{:S(2)}, u32[]{:S(2)}) collective-permute-start(bf16[1,160,640]{2,1,0:T(8,128)(2,1)S(1)} %get-tuple-element.32), channel_id=1, source_target_pairs={{16,8},{20,12},{24,16},{28,20},{17,9},{21,13},{25,17},{29,21},{18,... | collective-permute-start | bytes 614408 | tf_op jit(solution)/shard_map/ppermute | solution.py:505
  449.8 23.4 %collective-permute-start.8 = (bf16[1,160,640]{2,1,0:T(8,128)(2,1)S(1)}, bf16[1,160,640]{2,1,0:T(8,128)(2,1)S(1)}, u32[]{:S(2)}, u32[]{:S(2)}) collective-permute-start(bf16[1,160,640]{2,1,0:T(8,128)(2,1)S(1)} %get-tuple-element.31), channel_id=1, source_target_pairs={{16,12},{20,16},{24,20},{28,24},{17,13},{21,17},{25,21},{29,25},{1... | collective-permute-start | bytes 614408 | tf_op jit(solution)/shard_map/ppermute | solution.py:505
  477.3 1.2 copy-start.4

commit v3 on v2

--- a/solution.py
+++ b/solution.py
@@ -183,11 +183,12 @@
     )(role, bias, queries, keys_n, values)
 
 
-def spread_kernel(
-    x_ref, own_ref, oth_ref, xg_ref, wg_ref, relay_ref,
+def project_kernel(
+    x_ref, own_ref, oth_ref, gain_ref, q_ref, k_ref, v_ref,
+    xg_ref, wg_ref, relay_ref, total, sq, sq_in, sq_out,
     x_send, x_recv, near_send, near_recv, core_send, core_recv, pass_send, pass_recv,
-    mate_send, mate_recv, cross_send, relay_recv, fwd_send, a1_send, a1_recv, a2_send, a2_recv,
-    y_send, y_recv, local_sem,
+    cast_send, cast_recv, mate_send, mate_recv, cross_send, relay_recv, fwd_send, a1_send, a1_recv,
+    a2_send, a2_recv, y_send, y_recv, sum_send, sum_recv, local_sem,
 ):
     me, fs = lax.axis_index("seq"), lax.axis_index("fsdp")
     quarter, feats = x_ref.shape[1:]
@@ -211,9 +212,11 @@
         pl.semaphore_signal(
             barrier, inc=1, device_id=((me + r) % 8, fs), device_id_type=pl.DeviceIdType.MESH
         )
-    for f in (sib, across):
-        pl.semaphore_signal(barrier, inc=1, device_id=(me, f), device_id_type=pl.DeviceIdType.MESH)
-    pl.semaphore_wait(barrier, 9)
+    for r in range(1, 4):
+        pl.semaphore_signal(
+            barrier, inc=1, device_id=(me, (fs + r) % 4), device_id_type=pl.DeviceIdType.MESH
+        )
+    pl.semaphore_wait(barrier, 10)
 
     def remote(src, dst, send, recv, seq, fsdp):
         return pltpu.make_async_remote_copy(
@@ -289,7 +292,7 @@
     def keep_w(i):
         return pltpu.make_async_copy(own_ref.at[i], wg_ref.at[i, me], local_sem.at[i])
 
-    for i in range(kinds):
+    def start_w(i):
         mate_copy(i).start()
 
         @pl.when(outer)
@@ -302,6 +305,35 @@
 
         y_copy(i, 0).start()
         keep_w(i).start()
+
+    def forward_w(i):
+        mate_copy(i).wait_recv()
+        y_copy(i, 1).start()
+
+        @pl.when(inner)
+        def _():
+            relay_copy(i).wait_recv()
+            fwd_copy(i).start()
+
+        a1_copy(i).wait_recv()
+
+        @pl.when(inner)
+        def _():
+            a1_copy(i).start()
+
+        y_copy(i, 2).start()
+
+    def forward_last(i):
+        a2_copy(i).wait_recv()
+
+        @pl.when(inner)
+        def _():
+            a2_copy(i).start()
+
+        y_copy(i, 3).start()
+
+    start_w(0)
+    start_w(1)
 
     def near_copy(r):
         return remote(slot(r, fs), slot(r, fs), near_send.at[r], near_recv.at[r], me, across)
@@ -336,22 +368,9 @@
         near_copy(r).start()
         core_copy(r).start()
 
-    for i in range(kinds):
-        mate_copy(i).wait_recv()
-        y_copy(i, 1).start()
-
-        @pl.when(inner)
-        def _():
-            relay_copy(i).wait_recv()
-            fwd_copy(i).start()
-
-        a1_copy(i).wait_recv()
-
-        @pl.when(inner)
-        def _():
-            a1_copy(i).start()
-
-        y_copy(i, 2).start()
+    forward_w(0)
+    forward_w(1)
+    start_w(2)
 
     for r in range(8):
         remote(
@@ -359,21 +378,111 @@
         ).wait_recv()
         pass_copy(r).start()
 
-    for i in range(kinds):
-        a2_copy(i).wait_recv()
-
-        @pl.when(inner)
-        def _():
-            a2_copy(i).start()
-
-        y_copy(i, 3).start()
+    forward_last(0)
+    forward_last(1)
 
     for r in range(8):
         core_copy(r).wait_recv()
         pass_copy(r).wait_recv()
+
+    def multiply(i, k):
+        if k == 0:
+            keep_w(i).wait()
+        y_copy(i, k).wait_recv()
+        at_z = ((me, mate, a1, a2)[k]) // 2
+        cols = pl.ds(pl.multiple_of(at_z * feats, 128), feats)
+
+        def rows(t, carry):
+            at = pl.ds(t * half, half)
+            left = xg_ref[at, :, cols].reshape(half * quarter, feats)
+            right = wg_ref[i, pl.ds(at_z * 2, 2)].reshape(feats, wg_ref.shape[3])
+            term = jnp.dot(left, right, preferred_element_type=jnp.float32)
+            term = term.reshape(half, quarter, wg_ref.shape[3])
+            if k == 0:
+                total[i, at] = term
+            else:
+                total[i, at] = total[i, at] + term
+            return carry
+
+        lax.fori_loop(0, 2, rows, 0)
+
+    for k in range(3):
+        multiply(0, k)
+        multiply(1, k)
+    forward_w(2)
+    multiply(0, 3)
+    multiply(1, 3)
+
+    ones = jnp.ones((8, wg_ref.shape[3]), jnp.bfloat16)
+    last = (((1,), (1,)), ((), ()))
+
+    def sum_slot(r, carry):
+        for i in range(2):
+            raw = total[i, r]
+            square = raw * raw
+            high = square.astype(jnp.bfloat16)
+            low = (square - high.astype(jnp.float32)).astype(jnp.bfloat16)
+            found = lax.dot_general(ones, high, last, preferred_element_type=jnp.float32)
+            found = found + lax.dot_general(ones, low, last, preferred_element_type=jnp.float32)
+            sq[r, i] = jnp.concatenate(
+                [found, jnp.zeros((8, sq.shape[3] - quarter), jnp.float32)], axis=1
+            )
+        return carry
+
+    lax.fori_loop(0, 8, sum_slot, 0)
+
+    def cast_copy(p):
+        return remote(sq, sq_in.at[p], cast_send.at[p], cast_recv.at[p], me, (fs + p + 1) % 4)
+
+    for p in range(3):
+        cast_copy(p).start()
+    forward_last(2)
+    for k in range(2):
+        multiply(2, k)
+    for p in range(3):
+        cast_copy(p).wait_recv()
+    sq_out[...] = (sq[...] + sq_in[0]) + (sq_in[1] + sq_in[2])
+
+    def sum_copy(r):
+        frame_sp = me + r // half * half
+        part = r % half
+        to_t = half + part
+        at_t = (frame_sp + 2 * 8 - to_t) % 8
+        frame_tm = (me + r) % 8
+        to_s = frame_tm % half
+        at_s = frame_tm // half * half + me % half
+        target = jnp.where(is_spatial, to_t, to_s)
+        at = jnp.where(is_spatial, at_t, at_s)
+        return remote(sq_out.at[r], sq_in.at[3, at], sum_send.at[r], sum_recv.at[at], target, fs)
+
+    def sum_came(r):
+        return remote(sq_out.at[r], sq_in.at[3, r], sum_send.at[r], sum_recv.at[r], (me + 1) % 8, fs)
+
+    for r in range(8):
+        sum_copy(r).start()
+    for k in range(2, 4):
+        multiply(2, k)
+    for r in range(8):
+        sum_came(r).wait_recv()
+
+    def norm_slot(r, carry):
+        for i, out in ((0, q_ref), (1, k_ref)):
+            whole = sq_out[r, i] + sq_in[3, r, i]
+            scale = lax.rsqrt(whole / (H * HD) + 1e-06)
+            scale = jnp.transpose(scale)[:quarter, :1]
+            out[r] = (total[i, r] * scale * gain_ref[i]).astype(jnp.bfloat16)
+        v_ref[r] = total[2, r].astype(jnp.bfloat16)
+        return carry
+
+    lax.fori_loop(0, 8, norm_slot, 0)
+
+    for r in range(8):
+        sum_copy(r).wait_send()
         near_copy(r).wait_send()
         core_copy(r).wait_send()
         pass_copy(r).wait_send()
+    for p in range(3):
+        cast_copy(p).wait_send()
     for j in range(half):
         @pl.when(me != half + j)
         def _():
@@ -384,7 +493,6 @@
             to_spatial(j).wait_send()
 
     for i in range(kinds):
-        keep_w(i).wait()
         mate_copy(i).wait_send()
         cross_copy(i).wait_send()
 
@@ -395,31 +503,40 @@
             a2_copy(i).wait_send()
 
         for k in range(4):
-            y_copy(i, k).wait()
-
-
-def spread(x_quarters, w_own, w_oth, seq_count, fsdp_count):
+            y_copy(i, k).wait_send()
+
+
+def project(x_quarters, w_own, w_oth, gains, seq_count, fsdp_count):
     half, quarter, feats = x_quarters.shape
     kinds, rows, cols = w_own.shape
     dma = pltpu.SemaphoreType.DMA
     any_spec = pl.BlockSpec(memory_space=pl.ANY)
+    near = pl.BlockSpec(memory_space=pltpu.VMEM)
     sent = jnp.bfloat16
+    lanes = -(-quarter // 128) * 128
+    sums = (seq_count, 2, 8, lanes)
     return pl.pallas_call(
-        spread_kernel,
-        out_shape=[
-            jax.ShapeDtypeStruct((seq_count, quarter, feats * fsdp_count), sent),
-            jax.ShapeDtypeStruct((kinds, seq_count, rows, cols), sent),
-            jax.ShapeDtypeStruct((kinds, rows, cols), sent),
-        ],
-        in_specs=[any_spec] * 3,
-        out_specs=[any_spec] * 3,
-        scratch_shapes=[dma((8,))] * 8
+        project_kernel,
+        out_shape=[jax.ShapeDtypeStruct((seq_count, quarter, cols), sent)] * 3,
+        in_specs=[any_spec] * 3 + [near],
+        out_specs=[near] * 3,
+        scratch_shapes=[
+            pltpu.VMEM((seq_count, quarter, feats * fsdp_count), sent),
+            pltpu.VMEM((kinds, seq_count, rows, cols), sent),
+            pltpu.VMEM((kinds, rows, cols), sent),
+            pltpu.VMEM((kinds, seq_count, quarter, cols), jnp.float32),
+            pltpu.VMEM(sums, jnp.float32),
+            pltpu.VMEM((4,) + sums, jnp.float32),
+            pltpu.VMEM(sums, jnp.float32),
+        ]
+        + [dma((8,))] * 8
+        + [dma((3,))] * 2
         + [dma((kinds,))] * 9
-        + [dma((kinds, 4)), dma((kinds, 4)), dma((kinds + half,))],
+        + [dma((kinds, 4)), dma((kinds, 4)), dma((8,)), dma((8,)), dma((kinds + half,))],
         compiler_params=pltpu.CompilerParams(
-            collective_id=0, has_side_effects=True, vmem_limit_bytes=32 * 1024 * 1024
+            collective_id=0, has_side_effects=True, vmem_limit_bytes=60 * 1024 * 1024
         ),
-    )(x_quarters, w_own, w_oth)
+    )(x_quarters, w_own, w_oth, gains)
 
 
 def pick_heads(array, heads):
@@ -439,55 +556,29 @@
     quarter = rows // half
     head_count = head_kind.shape[0]
     kept = head_count // 2
-    order = jnp.argsort(head_kind, stable=True)
+    all_heads = jnp.arange(head_count)
+    kinds = (head_kind > 0).astype(jnp.int32)
+    before = all_heads[None, :] < all_heads[:, None]
+    tm_before = jnp.sum(jnp.where(before, kinds[None, :], 0), axis=1)
+    place = jnp.where(kinds > 0, kept + tm_before, all_heads - tm_before)
+    order = jnp.sum(
+        jnp.where(place[None, :] == all_heads[:, None], all_heads[None, :], 0), axis=1
+    )
     sp_heads = [order[i] for i in range(kept)]
     tm_heads = [order[kept + i] for i in range(kept)]
     my_heads = [jnp.where(is_spatial, s, t) for s, t in zip(sp_heads, tm_heads)]
 
     other_heads = [jnp.where(is_spatial, t, s) for s, t in zip(sp_heads, tm_heads)]
 
-    tokens, weights, _ = spread(
+    gains = jnp.stack([pick_heads(q_gain, my_heads), pick_heads(k_gain, my_heads)])
+    queries, keys_n, values = project(
         x_tokens.reshape(half, quarter, feats),
         pick_heads(w_qkv, my_heads),
         pick_heads(w_qkv, other_heads),
+        gains[:, None, :],
         seq_count,
         lax.axis_size("fsdp"),
     )
-    tokens = tokens.reshape(2 * rows, -1)
-    weights = weights.reshape(weights.shape[0], -1, kept * HD)
-    q_raw, k_raw, v_raw = [
-        jnp.dot(tokens, weights[i], preferred_element_type=jnp.float32) for i in range(3)
-    ]
-
-    sq = jnp.stack([jnp.sum(q_raw * q_raw, axis=1), jnp.sum(k_raw * k_raw, axis=1)])
-    sums = lax.all_gather(lax.psum(sq, "fsdp"), "seq", axis=0, tiled=False)
-    of_sp = sums[:half].reshape(half, 2, 2, rows).transpose(1, 2, 0, 3)
-    of_sp = of_sp.reshape(2, seq_count, rows)
-    of_tm = sums[half:].reshape(half, 2, seq_count, quarter).transpose(1, 2, 0, 3)
-    of_tm = jnp.stack(
-        [
-            jnp.take(of_tm[:, :, q], (jnp.arange(seq_count) - half - q) % seq_count, axis=1)
-            for q in range(half)
-        ],
-        axis=2,
-    ).reshape(2, seq_count, rows)
-    sums = of_sp + of_tm
-    sums_sp = jnp.take(sums, me % half + jnp.arange(2) * half, axis=1).reshape(2, 2 * rows)
-    pos_at = jnp.maximum(me - half, 0) * quarter
-    slot_at = (jnp.arange(seq_count) + me) % seq_count
-    sums_tm = jnp.take(
-        lax.dynamic_slice(sums, (0, 0, pos_at), (2, seq_count, quarter)), slot_at, axis=1
-    ).reshape(2, 2 * rows)
-    my_sums = jnp.where(is_spatial, sums_sp, sums_tm)
-
-    def normed(raw, total, gain):
-        gains = pick_heads(gain, my_heads)
-        scaled = raw * lax.rsqrt(total[:, None] / (H * HD) + 1e-06) * gains
-        return scaled.astype(jnp.bfloat16).reshape(seq_count, quarter, kept * HD)
-
-    queries = normed(q_raw, my_sums[0], q_gain)
-    keys_n = normed(k_raw, my_sums[1], k_gain)
-    values = v_raw.astype(jnp.bfloat16).reshape(seq_count, quarter, kept * HD)
 
     up_half = [(i + half, i) for i in range(half)]
     live = block_live[0]
@@ -510,7 +601,6 @@
     came_at = (me - half - jnp.arange(half)) % seq_count
     temporal = jnp.take(came, came_at, axis=0).reshape(rows, kept * HD)
     both = jnp.concatenate([spatial, temporal], axis=1)
-    place = jnp.argsort(order)
     return pick_heads(both, [place[h] for h in range(head_count)])
 
 

time: 480 us -> 404 us (0.84)
  blocking collectives: 72.1 us -> 0 us
  matrix products: 37.8 us -> 0 us
  Pallas kernels: 257 us -> 285 us
  starting transfers between devices: 19.3 us -> 35.4 us
  local copies, waits for them, and re-layouts: 44.2 us -> 36.4 us
  other arithmetic: 9.94 us -> 3.73 us
    all_gather x1 -> x0, blocking collectives: 61.9 us -> none  [split_shards(): sums = lax.all_gather(lax.psum(sq, 'fsdp'), 'seq', axis=0, tiled=False)]
    dot_general x3 -> x0, matrix products: 37.8 us -> none  [split_shards(): jnp.dot(tokens, weights[i], preferred_element_type=jnp.float32)]
    pallas_call x1, Pallas kernels: 235 us -> 263 us  [project(): pl.pallas_call(project_kernel, out_shape=[jax.ShapeDtypeStruct((seq_count...]
    ppermute x1, starting transfers between devices: 10.9 us -> 26.9 us  [split_shards(): lax.ppermute(done[half:], 'seq', [(i, i + half) for i in range(half)])]
    psum x1 -> x0, blocking collectives: 10.1 us -> none  [split_shards(): sums = lax.all_gather(lax.psum(sq, 'fsdp'), 'seq', axis=0, tiled=False)]
    slice x2 -> x0, local copies, waits for them, and re-layouts: 9.68 us -> none  [the longest x1 9.67 us: split_shards(): weights[i]]
  transfers between devices with their start and end apart: 9 -> 9, of which waited for: 4 -> 4; matrix products, arithmetic and copies ran while one was open for 17% -> 7% of each run, Pallas kernels for 49% -> 65%
where the time goes in v3:
time: 404 us; the launch traced here: 403 us
  Pallas kernels  285 us (71%)
  local copies, waits for them, and re-layouts  36.4 us (9%)
  starting transfers between devices  35.4 us (9%)
  waiting for transfers between devices  23.1 us (6%)
  between operations  19.3 us (5%)
    pallas_call x1, Pallas kernels, project(): pl.pallas_call(project_kernel, out_shape=[jax.ShapeDtypeStruct((seq_count...  263 us
    ppermute x1, starting transfers between devices, split_shards(): lax.ppermute(done[half:], 'seq', [(i, i + half) for i in range(half)])  26.9 us
    unnamed x29, local copies, waits for them, and re-layouts  25.9 us
    ppermute x7, waiting for transfers between devices, split_shards(): lax.ppermute(done[r:r + 1], 'seq', [(s, (s + r) % seq_count) for s in ran...  23.1 us
    pallas_call x1, Pallas kernels, attend(): pl.pallas_call(attend_kernel, grid=(cols // HD,), out_shape=jax.ShapeDtyp...  22.2 us
  transfers between devices with their start and end apart: 9, of which 4 were waited for; matrix products, arithmetic and copies ran while one was open for 7% of the time, Pallas kernels for 65%

profile of v3, /device:TPU:12, one launch (start us, length us, event | category | flops | bytes accessed | tf_op | source)
XLA Modules:
  0.0 403.0 jit_solution(14908005741680045201)
XLA Ops:
  0.7 1.3 collective-permute-start
  17.0 0.8 copy.16
  31.8 2.1 dynamic-slice_dynamic-update-slice_fusion.4
  33.9 2.2 dynamic-slice_dynamic-update-slice_fusion.3
  36.1 2.2 dynamic-slice_dynamic-update-slice_fusion.2
  38.3 2.2 dynamic-slice_dynamic-update-slice_fusion.1
  40.5 2.2 dynamic-slice_dynamic-update-slice_fusion
  44.2 263.0 %shard_map.64 = (bf16[8,160,640]{2,1,0:T(8,128)(2,1)}, bf16[8,160,640]{2,1,0:T(8,128)(2,1)}, bf16[8,160,640]{2,1,0:T(8,128)(2,1)}) custom-call(bf16[4,160,1280]{2,1,0:T(8,128)(2,1)} %bitcast.42, bf16[3,640,640]{2,1,0:T(8,128)(2,1)} %get-tuple-element.14.own_ref, bf16[3,640,640]{2,1,0:T(8,128)(2,1)} %copy-done.3, f32[2,1,640]{2,1,0:T(1,128)} %broadcast_in_dim.66.gain_ref), custom_call_target="tpu_custom_call" | custom-call | tf_op jit(solution)/shard_map/pallas_call | solution.py:518
  308.2 1.4 copy-done
  309.6 1.4 copy-done.1
  311.0 1.4 copy-done.2
  312.5 22.2 %shard_map.65 = bf16[8,160,640]{2,1,0:T(8,128)(2,1)S(1)} custom-call(s32[1]{0:T(128)} %bitcast.role_ref, f32[2,5,25]{2,1,0:T(8,128)S(1)} %fusion.20.bias_ref, bf16[8,160,640]{2,1,0:T(8,128)(2,1)S(1)} %copy-done, bf16[8,160,640]{2,1,0:T(8,128)(2,1)S(1)} %copy-done.1, bf16[8,160,640]{2,1,0:T(8,128)(2,1)S(1)} %copy-done.2), custom_call_target="tpu_custom_call" | custom-call | tf_op jit(solution)/shard_map/pallas_call | solution.py:170
  334.7 0.8 fusion.24
  336.9 26.9 %collective-permute-start.1 = (bf16[4,160,640]{2,1,0:T(8,128)(2,1)S(1)}, bf16[4,160,640]{2,1,0:T(8,128)(2,1)}, u32[]{:S(2)}, u32[]{:S(2)}) collective-permute-start(bf16[4,160,640]{2,1,0:T(8,128)(2,1)S(1)} %slice.129), channel_id=1, source_target_pairs={{0,16},{4,20},{8,24},{12,28},{1,17},{5,21},{9,25},{13,29},{2,18},{... | collective-permute-start | bytes 2457608 | tf_op jit(solution)/shard_map/ppermute | solution.py:591
  364.6 1.3 collective-permute-start.5
  365.9 1.3 collective-permute-start.6
  367.9 1.3 collective-permute-start.7
  369.9 1.3 collective-permute-start.8
  371.9 6.6 %collective-permute-done.5 = bf16[1,160,640]{2,1,0:T(8,128)(2,1)S(1)} collective-permute-done((bf16[1,160,640]{2,1,0:T(8,128)(2,1)S(1)}, bf16[1,160,640]{2,1,0:T(8,128)(2,1)S(1)}, u32[]{:S(2)}, u32[]{:S(2)}) %collective-permute-start.5) | collective-permute-done | bytes 204832 | tf_op jit(solution)/shard_map/ppermute | solution.py:596
  379.2 5.1 %collective-permute-done.6 = bf16[1,160,640]{2,1,0:T(8,128)(2,1)S(1)} collective-permute-done((bf16[1,160,640]{2,1,0:T(8,128)(2,1)S(1)}, bf16[1,160,640]{2,1,0:T(8,128)(2,1)S(1)}, u32[]{:S(2)}, u32[]{:S(2)}) %collective-permute-start.6) | collective-permute-done | bytes 204832 | tf_op jit(solution)/shard_map/ppermute | solution.py:596
  384.9 7.5 %collective-permute-done.7 = bf16[1,160,640]{2,1,0:T(8,128)(2,1)S(1)} collective-permute-done((bf16[1,160,640]{2,1,0:T(8,128)(2,1)S(1)}, bf16[1,160,640]{2,1,0:T(8,128)(2,1)S(1)}, u32[]{:S(2)}, u32[]{:S(2)}) %collective-permute-start.7) | collective-permute-done | bytes 204832 | tf_op jit(solution)/shard_map/ppermute | solution.py:596
  393.1 3.9 collective-permute-done.8
  397.7 2.1 gather_fusion.1
  401.1 1.2 copy-done.4
  (69 shorter events, 22.0 us)
Async XLA Ops:
  0.7 306.5 %collective-permute-start = (s32[10,5,5]{0,2,1:T(8,128)S(1)}, s32[10,5,5]{0,2,1:T(8,128)S(1)}, u32[]{:S(2)}, u32[]{:S(2)}) collective-permute-start(s32[10,5,5]{0,2,1:T(8,128)S(1)} %bitcast.45), channel_id=1, source_target_pairs={{16,0},{20,4},{24,8},{28,12},{17,1},{21,5},{25,9},{29,13},{18,2},{... | collective-permute-start | bytes 3008 | tf_op jit(solution)/shard_map/ppermute | solution.py:585
  42.7 1.5 copy-start.3
  308.2 1.4 copy-start
  309.6 1.4 copy-start.1
  311.0 1.4 copy-start.2
  335.5 30.4 %collective-permute-start.2 = (bf16[1,160,640]{2,1,0:T(8,128)(2,1)S(1)}, bf16[1,160,640]{2,1,0:T(8,128)(2,1)S(1)}, u32[]{:S(2)}, u32[]{:S(2)}) collective-permute-start(bf16[1,160,640]{2,1,0:T(8,128)(2,1)S(1)} %get-tuple-element.29), channel_id=1, source_target_pairs={{16,20},{20,24},{24,28},{28,0},{17,21},{21,25},{25,29},{29,1},{18,... | collective-permute-start | bytes 614408 | tf_op jit(solution)/shard_map/ppermute | solution.py:596
  336.2 31.7 %collective-permute-start.3 = (bf16[1,160,640]{2,1,0:T(8,128)(2,1)S(1)}, bf16[1,160,640]{2,1,0:T(8,128)(2,1)S(1)}, u32[]{:S(2)}, u32[]{:S(2)}) collective-permute-start(bf16[1,160,640]{2,1,0:T(8,128)(2,1)S(1)} %get-tuple-element.28), channel_id=1, source_target_pairs={{16,24},{20,28},{24,0},{28,4},{17,25},{21,29},{25,1},{29,5},{18,26... | collective-permute-start | bytes 614408 | tf_op jit(solution)/shard_map/ppermute | solution.py:596
  336.9 63.1 %collective-permute-start.1 = (bf16[4,160,640]{2,1,0:T(8,128)(2,1)S(1)}, bf16[4,160,640]{2,1,0:T(8,128)(2,1)}, u32[]{:S(2)}, u32[]{:S(2)}) collective-permute-start(bf16[4,160,640]{2,1,0:T(8,128)(2,1)S(1)} %slice.129), channel_id=1, source_target_pairs={{0,16},{4,20},{8,24},{12,28},{1,17},{5,21},{9,25},{13,29},{2,18},{... | collective-permute-start | bytes 2457608 | tf_op jit(solution)/shard_map/ppermute | solution.py:591
  363.9 6.0 %collective-permute-start.4 = (bf16[1,160,640]{2,1,0:T(8,128)(2,1)S(1)}, bf16[1,160,640]{2,1,0:T(8,128)(2,1)S(1)}, u32[]{:S(2)}, u32[]{:S(2)}) collective-permute-start(bf16[1,160,640]{2,1,0:T(8,128)(2,1)S(1)} %get-tuple-element.27), channel_id=1, source_target_pairs={{16,28},{20,0},{24,4},{28,8},{17,29},{21,1},{25,5},{29,9},{18,30},... | collective-permute-start | bytes 614408 | tf_op jit(solution)/shard_map/ppermute | solution.py:596
  364.6 13.9 %collective-permute-start.5 = (bf16[1,160,640]{2,1,0:T(8,128)(2,1)S(1)}, bf16[1,160,640]{2,1,0:T(8,128)(2,1)S(1)}, u32[]{:S(2)}, u32[]{:S(2)}) collective-permute-start(bf16[1,160,640]{2,1,0:T(8,128)(2,1)S(1)} %get-tuple-element.26), channel_id=1, source_target_pairs={{16,0},{20,4},{24,8},{28,12},{17,1},{21,5},{25,9},{29,13},{18,2},{... | collective-permute-start | bytes 614408 | tf_op jit(solution)/shard_map/ppermute | solution.py:596
  365.9 18.4 %collective-permute-start.6 = (bf16[1,160,640]{2,1,0:T(8,128)(2,1)S(1)}, bf16[1,160,640]{2,1,0:T(8,128)(2,1)S(1)}, u32[]{:S(2)}, u32[]{:S(2)}) collective-permute-start(bf16[1,160,640]{2,1,0:T(8,128)(2,1)S(1)} %get-tuple-element.25), channel_id=1, source_target_pairs={{16,4},{20,8},{24,12},{28,16},{17,5},{21,9},{25,13},{29,17},{18,6}... | collective-permute-start | bytes 614408 | tf_op jit(solution)/shard_map/ppermute | solution.py:596
  367.9 24.5 %collective-permute-start.7 = (bf16[1,160,640]{2,1,0:T(8,128)(2,1)S(1)}, bf16[1,160,640]{2,1,0:T(8,128)(2,1)S(1)}, u32[]{:S(2)}, u32[]{:S(2)}) collective-permute-start(bf16[1,160,640]{2,1,0:T(8,128)(2,1)S(1)} %get-tuple-element.24), channel_id=1, source_target_pairs={{16,8},{20,12},{24,16},{28,20},{17,9},{21,13},{25,17},{29,21},{18,... | collective-permute-start | bytes 614408 | tf_op jit(solution)/shard_map/ppermute | solution.py:596
  369.9 27.1 %collective-permute-start.8 = (bf16[1,160,640]{2,1,0:T(8,128)(2,1)S(1)}, bf16[1,160,640]{2,1,0:T(8,128)(2,1)S(1)}, u32[]{:S(2)}, u32[]{:S(2)}) collective-permute-start(bf16[1,160,640]{2,1,0:T(8,128)(2,1)S(1)} %get-tuple-element.23), channel_id=1, source_target_pairs={{16,12},{20,16},{24,20},{28,24},{17,13},{21,17},{25,21},{29,25},{1... | collective-permute-start | bytes 614408 | tf_op jit(solution)/shard_map/ppermute | solution.py:596
  401.1 1.2 copy-start.4

commit v4 on v3

--- a/solution.py
+++ b/solution.py
@@ -103,96 +103,18 @@
     is_temporal = jnp.repeat(head_kind > 0, HD)[None, :]
     return jnp.where(is_temporal, returned, spatial.reshape(tok_rows, col_width))
 
-def attend_kernel(role_ref, bias_ref, q_ref, k_ref, v_ref, out_ref):
-    head = pl.program_id(0)
-    score_scale = 1.0 / math.sqrt(HD)
-    slots, quarter, _ = q_ref.shape
-    frame_slots = slots // 2
-    frame_rows = frame_slots * quarter
-    blocks = frame_rows // BLK
-    contract_last = (((1,), (1,)), ((), ()))
-
-    def weigh(scores, vals):
-        row_max = jnp.max(scores, axis=-1, keepdims=True)
-        expo = jnp.exp(scores - row_max)
-        weights = (expo * (1.0 / jnp.sum(expo, axis=-1, keepdims=True))).astype(jnp.bfloat16)
-        return jnp.dot(weights, vals, preferred_element_type=jnp.float32).astype(jnp.bfloat16)
-
-    @pl.when(role_ref[0] == 1)
-    def _():
-        for frame in range(2):
-            at = pl.ds(frame * frame_slots, frame_slots)
-            qs = q_ref[at].reshape(frame_rows, HD)
-            ks = k_ref[at].reshape(frame_rows, HD)
-            vs = v_ref[at].reshape(frame_rows, HD)
-            pieces = []
-            for qb in range(blocks):
-                scores = (
-                    lax.dot_general(
-                        qs[qb * BLK : (qb + 1) * BLK],
-                        ks,
-                        contract_last,
-                        preferred_element_type=jnp.float32,
-                    )
-                    * score_scale
-                )
-                masked = [
-                    scores[:, kb * BLK : (kb + 1) * BLK]
-                    + bias_ref[frame, head, qb * blocks + kb]
-                    for kb in range(blocks)
-                ]
-                pieces.append(weigh(jnp.concatenate(masked, axis=1), vs))
-            out_ref[at] = jnp.concatenate(pieces, axis=0).reshape(frame_slots, quarter, HD)
-
-    @pl.when(role_ref[0] == 0)
-    def _():
-        step = 32
-        rows = slots * step
-        row_pos = lax.broadcasted_iota(jnp.int32, (rows, rows), 0) % step
-        col_pos = lax.broadcasted_iota(jnp.int32, (rows, rows), 1) % step
-        same = row_pos == col_pos
-        for pb in range(quarter // step):
-            at = pl.ds(pb * step, step)
-            qs = q_ref[:, at].reshape(rows, HD)
-            ks = k_ref[:, at].reshape(rows, HD)
-            vs = v_ref[:, at].reshape(rows, HD)
-            scores = (
-                lax.dot_general(qs, ks, contract_last, preferred_element_type=jnp.float32)
-                * score_scale
-            )
-            res = weigh(jnp.where(same, scores, -1e30), vs)
-            out_ref[:, at] = res.reshape(slots, step, HD)
-
-
-def attend(role, bias, queries, keys_n, values):
-    slots, quarter, cols = queries.shape
-    spec = pl.BlockSpec((slots, quarter, HD), lambda h: (0, 0, h))
-    return pl.pallas_call(
-        attend_kernel,
-        grid=(cols // HD,),
-        out_shape=jax.ShapeDtypeStruct(queries.shape, jnp.bfloat16),
-        in_specs=[
-            pl.BlockSpec(memory_space=pltpu.SMEM),
-            pl.BlockSpec(memory_space=pltpu.SMEM),
-            spec,
-            spec,
-            spec,
-        ],
-        out_specs=spec,
-        compiler_params=pltpu.CompilerParams(vmem_limit_bytes=40 * 1024 * 1024),
-    )(role, bias, queries, keys_n, values)
-
-
-def project_kernel(
-    x_ref, own_ref, oth_ref, gain_ref, q_ref, k_ref, v_ref,
-    xg_ref, wg_ref, relay_ref, total, sq, sq_in, sq_out,
+def block_kernel(
+    mask_ref, x_ref, w_ref, gain_ref, bias_ref, out_ref,
+    xg_ref, wg_ref, oth_ref, relay_ref, total, sq, sq_in, sq_out, bias_in, back,
     x_send, x_recv, near_send, near_recv, core_send, core_recv, pass_send, pass_recv,
     cast_send, cast_recv, mate_send, mate_recv, cross_send, relay_recv, fwd_send, a1_send, a1_recv,
-    a2_send, a2_recv, y_send, y_recv, sum_send, sum_recv, local_sem,
+    a2_send, a2_recv, y_send, y_recv, sum_send, sum_recv, local_sem, bias_send, bias_recv,
+    back_send, back_recv,
 ):
     me, fs = lax.axis_index("seq"), lax.axis_index("fsdp")
     quarter, feats = x_ref.shape[1:]
-    kinds = own_ref.shape[0]
+    kinds, _, width = oth_ref.shape
+    kept = width // HD
     half = 4
     z, y = me // 2, me % 2
     mate = (z + 1 - 2 * (z % 2)) * 2 + y
@@ -242,10 +164,10 @@
         )
 
     def keep_spatial(j):
-        return pltpu.make_async_copy(x_ref.at[j], slot(j, fs), local_sem.at[kinds + j])
+        return pltpu.make_async_copy(x_ref.at[j], slot(j, fs), local_sem.at[j])
 
     def keep_temporal():
-        return pltpu.make_async_copy(x_ref.at[me % half], slot(0, fs), local_sem.at[kinds])
+        return pltpu.make_async_copy(x_ref.at[me % half], slot(0, fs), local_sem.at[0])
 
     for j in range(half):
         @pl.when(me != half + j)
@@ -265,7 +187,7 @@
         keep_temporal().start()
 
     def mate_copy(i):
-        return remote(own_ref.at[i], wg_ref.at[i, me], mate_send.at[i], mate_recv.at[i], mate, fs)
+        return remote(wg_ref.at[i, me], wg_ref.at[i, me], mate_send.at[i], mate_recv.at[i], mate, fs)
 
     def relay_copy(i):
         return remote(oth_ref.at[i], relay_ref.at[i], cross_send.at[i], relay_recv.at[i], mate, fs)
@@ -286,11 +208,28 @@
 
     def y_copy(i, k):
         row = (me, mate, a1, a2)[k]
-        src = own_ref.at[i] if k == 0 else wg_ref.at[i, row]
-        return remote(src, wg_ref.at[i, row], y_send.at[i, k], y_recv.at[i, k], other_y, fs)
-
-    def keep_w(i):
-        return pltpu.make_async_copy(own_ref.at[i], wg_ref.at[i, me], local_sem.at[i])
+        at = wg_ref.at[i, row]
+        return remote(at, at, y_send.at[i, k], y_recv.at[i, k], other_y, fs)
+
+    heads = 2 * kept
+
+    def chosen_sum(first, blocks):
+        found = None
+        for h, block in blocks:
+            rows = block.shape[0] // mask_ref.shape[1]
+            term = block.reshape(rows, *mask_ref.shape[1:]) * mask_ref[first + h][None]
+            found = term if found is None else found + term
+        return found.reshape(-1, HD)
+
+    def pick_w(i):
+        def cut(h):
+            return w_ref[i, :, pl.ds(h * HD, HD)]
+
+        for n in range(kept):
+            near_heads = range(n, n + kept + 1)
+            to = pl.ds(n * HD, HD)
+            wg_ref[i, me, :, to] = chosen_sum(n * heads, [(h, cut(h)) for h in near_heads])
+            oth_ref[i, :, to] = chosen_sum((kept + n) * heads, [(h, cut(h)) for h in near_heads])
 
     def start_w(i):
         mate_copy(i).start()
@@ -304,7 +243,6 @@
             cross_copy(i).start()
 
         y_copy(i, 0).start()
-        keep_w(i).start()
 
     def forward_w(i):
         mate_copy(i).wait_recv()
@@ -332,8 +270,18 @@
 
         y_copy(i, 3).start()
 
+    pick_w(0)
     start_w(0)
+    pick_w(1)
     start_w(1)
+    pick_w(2)
+
+    def bias_copy():
+        return remote(bias_ref, bias_in, bias_send, bias_recv, (me + half) % 8, fs)
+
+    @pl.when(is_temporal)
+    def _():
+        bias_copy().start()
 
     def near_copy(r):
         return remote(slot(r, fs), slot(r, fs), near_send.at[r], near_recv.at[r], me, across)
@@ -386,8 +334,6 @@
         pass_copy(r).wait_recv()
 
     def multiply(i, k):
-        if k == 0:
-            keep_w(i).wait()
         y_copy(i, k).wait_recv()
         at_z = ((me, mate, a1, a2)[k]) // 2
         cols = pl.ds(pl.multiple_of(at_z * feats, 128), feats)
@@ -465,22 +411,142 @@
     for r in range(8):
         sum_came(r).wait_recv()
 
+    for r in range(8):
+        near_copy(r).wait_send()
+        core_copy(r).wait_send()
+        pass_copy(r).wait_send()
+
     def norm_slot(r, carry):
-        for i, out in ((0, q_ref), (1, k_ref)):
+        for i in range(2):
             whole = sq_out[r, i] + sq_in[3, r, i]
             scale = lax.rsqrt(whole / (H * HD) + 1e-06)
             scale = jnp.transpose(scale)[:quarter, :1]
-            out[r] = (total[i, r] * scale * gain_ref[i]).astype(jnp.bfloat16)
-        v_ref[r] = total[2, r].astype(jnp.bfloat16)
+            normed = (total[i, r] * scale * gain_ref[i]).astype(jnp.bfloat16)
+            xg_ref[r, :, pl.ds(i * width, width)] = normed
+        xg_ref[r, :, pl.ds(2 * width, width)] = total[2, r].astype(jnp.bfloat16)
         return carry
 
     lax.fori_loop(0, 8, norm_slot, 0)
+
+    factor = math.log2(math.e) / math.sqrt(HD)
+
+    def head_cols(i, h):
+        return pl.ds(pl.multiple_of(i * width + h * HD, HD), HD)
+
+    def weigh(scores, vals):
+        row_max = jnp.max(scores, axis=-1, keepdims=True)
+        expo = jnp.exp2(scores - row_max)
+        inverse = 1.0 / jnp.sum(expo, axis=-1, keepdims=True)
+        mixed = jnp.dot(expo.astype(jnp.bfloat16), vals, preferred_element_type=jnp.float32)
+        return (mixed * inverse).astype(jnp.bfloat16)
+
+    frame_rows = half * quarter
+
+    def spatial_frame(frame, mask_ref):
+        at = pl.ds(frame * half, half)
+
+        def one_head(h, carry):
+            qs, ks, vs = [
+                xg_ref[at, :, head_cols(i, h)].reshape(frame_rows, HD) for i in range(3)
+            ]
+            pieces = []
+            for qb in range(frame_rows // BLK):
+                scores = lax.dot_general(
+                    qs[qb * BLK : (qb + 1) * BLK], ks, last, preferred_element_type=jnp.float32
+                )
+                pieces.append(weigh(scores * factor + mask_ref[h, pl.ds(qb, 1)], vs))
+            res = jnp.concatenate(pieces, axis=0).reshape(half, quarter, HD)
+            if frame == 0:
+                back[:, :, head_cols(0, h)] = res
+            else:
+                xg_ref[at, :, head_cols(3, h)] = res
+            return carry
+
+        lax.fori_loop(0, kept, one_head, 0)
+
+    step = 32
+    mix = 8 * step
+
+    def temporal_all():
+        row_pos = lax.broadcasted_iota(jnp.int32, (mix, mix), 0) % step
+        col_pos = lax.broadcasted_iota(jnp.int32, (mix, mix), 1) % step
+        hide = jnp.where(row_pos == col_pos, 0.0, -1e30)
+
+        def one_head(h, carry):
+            for pb in range(quarter // step):
+                at = pl.ds(pb * step, step)
+                qs, ks, vs = [
+                    xg_ref[:, at, head_cols(i, h)].reshape(mix, HD) for i in range(3)
+                ]
+                scores = lax.dot_general(qs, ks, last, preferred_element_type=jnp.float32)
+                res = weigh(scores * factor + hide, vs)
+                xg_ref[:, at, head_cols(3, h)] = res.reshape(8, step, HD)
+            return carry
+
+        lax.fori_loop(0, kept, one_head, 0)
+
+    def back_spatial():
+        return remote(
+            xg_ref.at[pl.ds(half, half), :, pl.ds(3 * width, width)],
+            back.at[:, :, pl.ds(0, width)],
+            back_send.at[0], back_recv.at[0], (me + half) % 8, fs,
+        )
+
+    def back_temporal(r):
+        return remote(
+            xg_ref.at[r, :, pl.ds(3 * width, width)],
+            back.at[me % half, :, pl.ds(width, width)],
+            back_send.at[r], back_recv.at[1 + me % half], (me + r) % 8, fs,
+        )
+
+    def back_came(q):
+        return remote(
+            xg_ref.at[0, :, pl.ds(3 * width, width)],
+            back.at[q, :, pl.ds(width, width)],
+            back_send.at[0], back_recv.at[1 + q], (me + 1) % 8, fs,
+        )
+
+    @pl.when(is_spatial)
+    def _():
+        bias_copy().wait_recv()
+        spatial_frame(1, bias_in)
+        back_spatial().start()
+        spatial_frame(0, bias_ref)
+
+    @pl.when(is_temporal)
+    def _():
+        temporal_all()
+        for r in range(1, 8):
+            back_temporal(r).start()
+        back[me % half, :, pl.ds(width, width)] = xg_ref[0, :, pl.ds(3 * width, width)]
+        bias_copy().wait_send()
+        back_spatial().wait_recv()
+
+    for q in range(half):
+        @pl.when(me != half + q)
+        def _():
+            back_came(q).wait_recv()
+
+    for h in range(heads):
+        ranks = [n for n in range(kept) if n <= h <= n + kept]
+        blocks = [
+            (p, back[:, :, pl.ds(p * HD, HD)].reshape(frame_rows, HD))
+            for p in ranks + [kept + n for n in ranks]
+        ]
+        res = chosen_sum((heads + h) * heads, blocks)
+        out_ref[:, :, pl.ds(h * HD, HD)] = res.reshape(half, quarter, HD)
+
+    @pl.when(is_spatial)
+    def _():
+        back_spatial().wait_send()
+
+    @pl.when(is_temporal)
+    def _():
+        for r in range(1, 8):
+            back_temporal(r).wait_send()
 
     for r in range(8):
         sum_copy(r).wait_send()
-        near_copy(r).wait_send()
-        core_copy(r).wait_send()
-        pass_copy(r).wait_send()
     for p in range(3):
         cast_copy(p).wait_send()
     for j in range(half):
@@ -506,51 +572,53 @@
             y_copy(i, k).wait_send()
 
 
-def project(x_quarters, w_own, w_oth, gains, seq_count, fsdp_count):
+def attend_block(masks, x_quarters, w_qkv, gains, bias, seq_count, fsdp_count):
     half, quarter, feats = x_quarters.shape
-    kinds, rows, cols = w_own.shape
+    kinds, rows, _ = w_qkv.shape
+    cols = gains.shape[-1]
     dma = pltpu.SemaphoreType.DMA
-    any_spec = pl.BlockSpec(memory_space=pl.ANY)
     near = pl.BlockSpec(memory_space=pltpu.VMEM)
     sent = jnp.bfloat16
     lanes = -(-quarter // 128) * 128
     sums = (seq_count, 2, 8, lanes)
     return pl.pallas_call(
-        project_kernel,
-        out_shape=[jax.ShapeDtypeStruct((seq_count, quarter, cols), sent)] * 3,
-        in_specs=[any_spec] * 3 + [near],
-        out_specs=[near] * 3,
+        block_kernel,
+        out_shape=jax.ShapeDtypeStruct((half, quarter, 2 * cols), sent),
+        in_specs=[
+            near,
+            pl.BlockSpec(memory_space=pl.ANY),
+            near,
+            near,
+            near,
+        ],
+        out_specs=near,
         scratch_shapes=[
             pltpu.VMEM((seq_count, quarter, feats * fsdp_count), sent),
             pltpu.VMEM((kinds, seq_count, rows, cols), sent),
+            pltpu.VMEM((kinds, rows, cols), sent),
             pltpu.VMEM((kinds, rows, cols), sent),
             pltpu.VMEM((kinds, seq_count, quarter, cols), jnp.float32),
             pltpu.VMEM(sums, jnp.float32),
             pltpu.VMEM((4,) + sums, jnp.float32),
             pltpu.VMEM(sums, jnp.float32),
+            pltpu.VMEM(bias.shape, jnp.float32),
+            pltpu.VMEM((half, quarter, 2 * cols), sent),
         ]
         + [dma((8,))] * 8
         + [dma((3,))] * 2
         + [dma((kinds,))] * 9
-        + [dma((kinds, 4)), dma((kinds, 4)), dma((8,)), dma((8,)), dma((kinds + half,))],
+        + [dma((kinds, 4)), dma((kinds, 4)), dma((8,)), dma((8,)), dma((half,))]
+        + [dma, dma, dma((8,)), dma((8,))],
         compiler_params=pltpu.CompilerParams(
-            collective_id=0, has_side_effects=True, vmem_limit_bytes=60 * 1024 * 1024
+            collective_id=0, has_side_effects=True, vmem_limit_bytes=61 * 1024 * 1024
         ),
-    )(x_quarters, w_own, w_oth, gains)
-
-
-def pick_heads(array, heads):
-    return jnp.concatenate(
-        [lax.dynamic_slice_in_dim(array, head * HD, HD, axis=array.ndim - 1) for head in heads],
-        axis=-1,
-    )
+    )(masks, x_quarters, w_qkv, gains, bias)
 
 
 def split_shards(x_tokens, w_qkv, q_gain, k_gain, head_kind, block_live):
     seq_count = lax.axis_size("seq")
     half = seq_count // 2
     me = lax.axis_index("seq")
-    z, y = me // 2, me % 2
     is_spatial = me < half
     rows, feats = x_tokens.shape
     quarter = rows // half
@@ -564,44 +632,32 @@
     order = jnp.sum(
         jnp.where(place[None, :] == all_heads[:, None], all_heads[None, :], 0), axis=1
     )
-    sp_heads = [order[i] for i in range(kept)]
-    tm_heads = [order[kept + i] for i in range(kept)]
-    my_heads = [jnp.where(is_spatial, s, t) for s, t in zip(sp_heads, tm_heads)]
-
-    other_heads = [jnp.where(is_spatial, t, s) for s, t in zip(sp_heads, tm_heads)]
-
-    gains = jnp.stack([pick_heads(q_gain, my_heads), pick_heads(k_gain, my_heads)])
-    queries, keys_n, values = project(
+    flip = jnp.where(is_spatial, 0, kept)
+    slots = jnp.arange(head_count)
+    wanted = jnp.where(slots[:, None] == (slots[None, :] + flip) % head_count, order[:, None], 0)
+    ordered = jnp.sum(wanted, axis=0)
+    mine = ordered[:kept, None] == all_heads[None, :]
+    both_gains = jnp.stack([q_gain, k_gain]).reshape(2, 1, head_count, HD)
+    gains = jnp.sum(jnp.where(mine[None, :, :, None], both_gains, 0.0), axis=2)
+    live = block_live[0].astype(jnp.float32)
+    chosen = order[:kept, None] == all_heads[None, :]
+    live = jnp.sum(jnp.where(chosen[:, :, None, None], live[None], 0.0), axis=1)
+    bias = jnp.repeat(jnp.where(live > 0, 0.0, -1e30), BLK, axis=2)
+    bias = jnp.pad(bias, ((0, 0), (0, -bias.shape[1] % 8), (0, 0)))
+    at_heads = jnp.concatenate([ordered, place])[:, None] == all_heads[None, :]
+    masks = jnp.broadcast_to(
+        at_heads.astype(jnp.bfloat16).reshape(-1, 1, 1), (at_heads.size, 16, HD)
+    )
+    done = attend_block(
+        masks,
         x_tokens.reshape(half, quarter, feats),
-        pick_heads(w_qkv, my_heads),
-        pick_heads(w_qkv, other_heads),
-        gains[:, None, :],
+        w_qkv,
+        gains.reshape(2, 1, kept * HD),
+        bias,
         seq_count,
         lax.axis_size("fsdp"),
     )
-
-    up_half = [(i + half, i) for i in range(half)]
-    live = block_live[0]
-    live_two = jnp.stack([live, lax.ppermute(live, "seq", up_half)])
-    live_two = jnp.take(live_two, order[:kept], axis=1)
-    bias = jnp.where(live_two.reshape(2, kept, -1) > 0, 0.0, -1e30).astype(jnp.float32)
-    role = is_spatial.astype(jnp.int32).reshape(1)
-    done = attend(role, bias, queries, keys_n, values)
-
-    back = lax.ppermute(done[half:], "seq", [(i, i + half) for i in range(half)])
-    spatial = jnp.where(is_spatial, done[:half], back).reshape(rows, kept * HD)
-    came = [done[:1]]
-    for r in range(1, seq_count):
-        came.append(
-            lax.ppermute(
-                done[r : r + 1], "seq", [(s, (s + r) % seq_count) for s in range(half, seq_count)]
-            )
-        )
-    came = jnp.concatenate(came, axis=0)
-    came_at = (me - half - jnp.arange(half)) % seq_count
-    temporal = jnp.take(came, came_at, axis=0).reshape(rows, kept * HD)
-    both = jnp.concatenate([spatial, temporal], axis=1)
-    return pick_heads(both, [place[h] for h in range(head_count)])
+    return done.reshape(rows, head_count * HD)
 
 
 def solution(mesh):

time: 404 us -> 338 us (0.84)
  Pallas kernels: 285 us -> 324 us
  starting transfers between devices: 35.4 us -> 0 us
  local copies, waits for them, and re-layouts: 36.4 us -> 6.74 us
  waiting for transfers between devices: 23.1 us -> 0 us
  between operations: 19.3 us -> 0.07 us
    pallas_call x2 -> x1, Pallas kernels: 285 us -> 324 us  [attend_block(): pl.pallas_call(block_kernel, out_shape=jax.ShapeDtypeStruct((half, quarte...]
    ppermute x9 -> x0, starting transfers between devices: 35.4 us -> none  [the longest x1 26.9 us: split_shards(): lax.ppermute(done[half:], 'seq', [(i, i + half) for i in range(half)])]
    unnamed x29 -> x2, local copies, waits for them, and re-layouts: 25.9 us -> 2.7 us
    ppermute x9 -> x0, waiting for transfers between devices: 23.1 us -> none  [the longest x7 23.1 us: split_shards(): lax.ppermute(done[r:r + 1], 'seq', [(s, (s + r) % seq_count) for s in ran...]
    concatenate x4 -> x0, local copies, waits for them, and re-layouts: 4.45 us -> none  [the longest x3 3.75 us: pick_heads(): jnp.concatenate([lax.dynamic_slice_in_dim(array, head * HD, HD, axis=arra...]
  transfers between devices with their start and end apart: 9 -> 0, of which waited for: 4 -> 0; matrix products, arithmetic and copies ran while one was open for 7% -> 0% of each run, Pallas kernels for 65% -> 0%
where the time goes in v4:
time: 338 us; the launch traced here: 333 us
  Pallas kernels  324 us (96%)
  local copies, waits for them, and re-layouts  6.74 us (2%)
    pallas_call x1, Pallas kernels, attend_block(): pl.pallas_call(block_kernel, out_shape=jax.ShapeDtypeStruct((half, quarte...  324 us

profile of v4, /device:TPU:12, one launch (start us, length us, event | category | flops | bytes accessed | tf_op | source)
XLA Modules:
  0.0 333.4 jit_solution(12339834117829562962)
XLA Ops:
  0.0 0.7 compare_convert_fusion
  0.7 0.1 select_reduce_fusion.4
  0.8 0.7 compare_select_fusion.1
  1.5 0.1 select_reduce_fusion.3
  1.6 0.1 select_reduce_fusion.2
  1.7 0.1 pad_add_fusion
  1.7 0.1 iota_compare_fusion.4
  1.8 0.1 iota_compare_fusion.5
  1.9 0.7 stack.9
  2.6 0.7 stack.10
  3.3 0.1 select_reduce_fusion.1
  3.4 0.6 copy.10.gain_ref
  4.0 0.1 fusion
  4.1 0.1 reshape.102
  4.2 0.7 convert_element_type.22
  5.0 0.1 select_reduce_fusion
  5.1 0.1 broadcast_in_dim.115
  5.2 0.6 pad.4.bias_ref
  5.8 1.2 broadcast_in_dim.105.mask_ref
  7.0 323.7 %shard_map.64 = bf16[4,160,1280]{2,1,0:T(8,128)(2,1)} custom-call(bf16[200,16,128]{2,1,0:T(8,128)(2,1)} %broadcast_in_dim.105.mask_ref, bf16[4,160,1280]{2,1,0:T(8,128)(2,1)} %bitcast.11, bf16[3,640,1280]{2,1,0:T(8,128)(2,1)} %w_ref.1, f32[2,1,640]{2,1,0:T(1,128)} %copy.10.gain_ref, f32[5,8,640]{2,1,0:T(8,128)} %pad.4.bias_ref), custom_call_target="tpu_custom_call" | custom-call | tf_op jit(solution)/shard_map/pallas_call | solution.py:584
  330.7 2.7 copy.15
  (5 shorter events, 0.1 us)

commit v5 on v4

--- a/solution.py
+++ b/solution.py
@@ -186,30 +186,41 @@
     def _():
         keep_temporal().start()
 
-    def mate_copy(i):
-        return remote(wg_ref.at[i, me], wg_ref.at[i, me], mate_send.at[i], mate_recv.at[i], mate, fs)
-
-    def relay_copy(i):
-        return remote(oth_ref.at[i], relay_ref.at[i], cross_send.at[i], relay_recv.at[i], mate, fs)
-
-    def cross_copy(i):
-        return remote(oth_ref.at[i], wg_ref.at[i, me], cross_send.at[i], a1_recv.at[i], a1, fs)
-
-    def fwd_copy(i):
-        return remote(relay_ref.at[i], wg_ref.at[i, mate], fwd_send.at[i], a2_recv.at[i], a1, fs)
-
-    def a1_copy(i):
-        at = wg_ref.at[i, a1]
-        return remote(at, at, a1_send.at[i], a1_recv.at[i], mate, fs)
-
-    def a2_copy(i):
-        at = wg_ref.at[i, a2]
-        return remote(at, at, a2_send.at[i], a2_recv.at[i], mate, fs)
-
-    def y_copy(i, k):
-        row = (me, mate, a1, a2)[k]
-        at = wg_ref.at[i, row]
-        return remote(at, at, y_send.at[i, k], y_recv.at[i, k], other_y, fs)
+    early = (kept + 1) // 2
+    cut_at = early * HD
+    parts = ((0, 0, width), (1, 0, width), (2, 0, cut_at), (2, cut_at, width - cut_at))
+
+    def held(c, row):
+        i, low, size = parts[c]
+        return wg_ref.at[i, row, :, pl.ds(low, size)]
+
+    def loose(ref, c):
+        i, low, size = parts[c]
+        return ref.at[i, :, pl.ds(low, size)]
+
+    def mate_copy(c):
+        return remote(held(c, me), held(c, me), mate_send.at[c], mate_recv.at[c], mate, fs)
+
+    def relay_copy(c):
+        return remote(
+            loose(oth_ref, c), loose(relay_ref, c), cross_send.at[c], relay_recv.at[c], mate, fs
+        )
+
+    def cross_copy(c):
+        return remote(loose(oth_ref, c), held(c, me), cross_send.at[c], a1_recv.at[c], a1, fs)
+
+    def fwd_copy(c):
+        return remote(loose(relay_ref, c), held(c, mate), fwd_send.at[c], a2_recv.at[c], a1, fs)
+
+    def a1_copy(c):
+        return remote(held(c, a1), held(c, a1), a1_send.at[c], a1_recv.at[c], mate, fs)
+
+    def a2_copy(c):
+        return remote(held(c, a2), held(c, a2), a2_send.at[c], a2_recv.at[c], mate, fs)
+
+    def y_copy(c, k):
+        at = held(c, (me, mate, a1, a2)[k])
+        return remote(at, at, y_send.at[c, k], y_recv.at[c, k], other_y, fs)
 
     heads = 2 * kept
 
@@ -319,6 +330,7 @@
     forward_w(0)
     forward_w(1)
     start_w(2)
+    start_w(3)
 
     for r in range(8):
         remote(
@@ -333,24 +345,39 @@
         core_copy(r).wait_recv()
         pass_copy(r).wait_recv()
 
-    def multiply(i, k):
-        y_copy(i, k).wait_recv()
+    def multiply(c, k):
+        i, low, size = parts[c]
+        y_copy(c, k).wait_recv()
         at_z = ((me, mate, a1, a2)[k]) // 2
         cols = pl.ds(pl.multiple_of(at_z * feats, 128), feats)
+        to = pl.ds(low, size)
 
         def rows(t, carry):
             at = pl.ds(t * half, half)
             left = xg_ref[at, :, cols].reshape(half * quarter, feats)
-            right = wg_ref[i, pl.ds(at_z * 2, 2)].reshape(feats, wg_ref.shape[3])
+            right = wg_ref[i, pl.ds(at_z * 2, 2), :, to].reshape(feats, size)
             term = jnp.dot(left, right, preferred_element_type=jnp.float32)
-            term = term.reshape(half, quarter, wg_ref.shape[3])
+            term = term.reshape(half, quarter, size)
             if k == 0:
-                total[i, at] = term
+                total[i, at, :, to] = term
             else:
-                total[i, at] = total[i, at] + term
+                total[i, at, :, to] = total[i, at, :, to] + term
             return carry
 
         lax.fori_loop(0, 2, rows, 0)
+
+    def sent_w(c):
+        mate_copy(c).wait_send()
+        cross_copy(c).wait_send()
+
+        @pl.when(inner)
+        def _():
+            fwd_copy(c).wait_send()
+            a1_copy(c).wait_send()
+            a2_copy(c).wait_send()
+
+        for k in range(4):
+            y_copy(c, k).wait_send()
 
     for k in range(3):
         multiply(0, k)
@@ -383,6 +410,7 @@
     for p in range(3):
         cast_copy(p).start()
     forward_last(2)
+    forward_w(3)
     for k in range(2):
         multiply(2, k)
     for p in range(3):
@@ -411,10 +439,10 @@
     for r in range(8):
         sum_came(r).wait_recv()
 
-    for r in range(8):
-        near_copy(r).wait_send()
-        core_copy(r).wait_send()
-        pass_copy(r).wait_send()
+    sent_w(0)
+
+    def held_rows(i):
+        return pl.ds(i * quarter, quarter)
 
     def norm_slot(r, carry):
         for i in range(2):
@@ -422,16 +450,31 @@
             scale = lax.rsqrt(whole / (H * HD) + 1e-06)
             scale = jnp.transpose(scale)[:quarter, :1]
             normed = (total[i, r] * scale * gain_ref[i]).astype(jnp.bfloat16)
-            xg_ref[r, :, pl.ds(i * width, width)] = normed
-        xg_ref[r, :, pl.ds(2 * width, width)] = total[2, r].astype(jnp.bfloat16)
+            wg_ref[0, r, held_rows(i)] = normed
         return carry
 
     lax.fori_loop(0, 8, norm_slot, 0)
 
+    def round_values(c):
+        _, low, size = parts[c]
+
+        def value_slot(r, carry):
+            found = total[2, r, :, pl.ds(low, size)]
+            wg_ref[0, r, held_rows(2), pl.ds(low, size)] = found.astype(jnp.bfloat16)
+            return carry
+
+        lax.fori_loop(0, 8, value_slot, 0)
+
     factor = math.log2(math.e) / math.sqrt(HD)
 
-    def head_cols(i, h):
-        return pl.ds(pl.multiple_of(i * width + h * HD, HD), HD)
+    def head_cols(h):
+        return pl.ds(pl.multiple_of(h * HD, HD), HD)
+
+    group_heads = ((0, early), (early, kept))
+
+    def group_cols(g, first=0):
+        low, high = group_heads[g]
+        return pl.ds(first + low * HD, (high - low) * HD)
 
     def weigh(scores, vals):
         row_max = jnp.max(scores, axis=-1, keepdims=True)
@@ -442,12 +485,13 @@
 
     frame_rows = half * quarter
 
-    def spatial_frame(frame, mask_ref):
+    def spatial_frame(frame, mask_ref, g):
         at = pl.ds(frame * half, half)
 
         def one_head(h, carry):
             qs, ks, vs = [
-                xg_ref[at, :, head_cols(i, h)].reshape(frame_rows, HD) for i in range(3)
+                wg_ref[0, at, held_rows(i), head_cols(h)].reshape(frame_rows, HD)
+                for i in range(3)
             ]
             pieces = []
             for qb in range(frame_rows // BLK):
@@ -457,75 +501,99 @@
                 pieces.append(weigh(scores * factor + mask_ref[h, pl.ds(qb, 1)], vs))
             res = jnp.concatenate(pieces, axis=0).reshape(half, quarter, HD)
             if frame == 0:
-                back[:, :, head_cols(0, h)] = res
+                back[:, :, head_cols(h)] = res
             else:
-                xg_ref[at, :, head_cols(3, h)] = res
+                wg_ref[0, at, held_rows(3), head_cols(h)] = res
             return carry
 
-        lax.fori_loop(0, kept, one_head, 0)
+        lax.fori_loop(*group_heads[g], one_head, 0)
 
     step = 32
     mix = 8 * step
 
-    def temporal_all():
+    def temporal_all(g):
         row_pos = lax.broadcasted_iota(jnp.int32, (mix, mix), 0) % step
         col_pos = lax.broadcasted_iota(jnp.int32, (mix, mix), 1) % step
         hide = jnp.where(row_pos == col_pos, 0.0, -1e30)
 
         def one_head(h, carry):
             for pb in range(quarter // step):
-                at = pl.ds(pb * step, step)
                 qs, ks, vs = [
-                    xg_ref[:, at, head_cols(i, h)].reshape(mix, HD) for i in range(3)
+                    wg_ref[0, :, pl.ds(i * quarter + pb * step, step), head_cols(h)].reshape(mix, HD)
+                    for i in range(3)
                 ]
                 scores = lax.dot_general(qs, ks, last, preferred_element_type=jnp.float32)
                 res = weigh(scores * factor + hide, vs)
-                xg_ref[:, at, head_cols(3, h)] = res.reshape(8, step, HD)
+                to = pl.ds(3 * quarter + pb * step, step)
+                wg_ref[0, :, to, head_cols(h)] = res.reshape(8, step, HD)
             return carry
 
-        lax.fori_loop(0, kept, one_head, 0)
-
-    def back_spatial():
+        lax.fori_loop(*group_heads[g], one_head, 0)
+
+    def back_spatial(g):
         return remote(
-            xg_ref.at[pl.ds(half, half), :, pl.ds(3 * width, width)],
-            back.at[:, :, pl.ds(0, width)],
-            back_send.at[0], back_recv.at[0], (me + half) % 8, fs,
-        )
-
-    def back_temporal(r):
+            wg_ref.at[0, pl.ds(half, half), held_rows(3), group_cols(g)],
+            back.at[:, :, group_cols(g)],
+            back_send.at[g, 0], back_recv.at[g, 0], (me + half) % 8, fs,
+        )
+
+    def back_temporal(g, r):
         return remote(
-            xg_ref.at[r, :, pl.ds(3 * width, width)],
-            back.at[me % half, :, pl.ds(width, width)],
-            back_send.at[r], back_recv.at[1 + me % half], (me + r) % 8, fs,
-        )
-
-    def back_came(q):
+            wg_ref.at[0, r, held_rows(3), group_cols(g)],
+            back.at[me % half, :, group_cols(g, width)],
+            back_send.at[g, r], back_recv.at[g, 1 + me % half], (me + r) % 8, fs,
+        )
+
+    def back_came(g, q):
         return remote(
-            xg_ref.at[0, :, pl.ds(3 * width, width)],
-            back.at[q, :, pl.ds(width, width)],
-            back_send.at[0], back_recv.at[1 + q], (me + 1) % 8, fs,
-        )
-
-    @pl.when(is_spatial)
-    def _():
-        bias_copy().wait_recv()
-        spatial_frame(1, bias_in)
-        back_spatial().start()
-        spatial_frame(0, bias_ref)
+            wg_ref.at[0, 0, held_rows(3), group_cols(g)],
+            back.at[q, :, group_cols(g, width)],
+            back_send.at[g, 0], back_recv.at[g, 1 + q], (me + 1) % 8, fs,
+        )
+
+    def attend_first(g):
+        @pl.when(is_spatial)
+        def _():
+            if g == 0:
+                bias_copy().wait_recv()
+            spatial_frame(1, bias_in, g)
+            back_spatial(g).start()
+
+        @pl.when(is_temporal)
+        def _():
+            temporal_all(g)
+            for r in range(1, 8):
+                back_temporal(g, r).start()
+            back[me % half, :, group_cols(g, width)] = wg_ref[0, 0, held_rows(3), group_cols(g)]
+
+    def attend_rest(g):
+        @pl.when(is_spatial)
+        def _():
+            spatial_frame(0, bias_ref, g)
+
+    round_values(2)
+    attend_first(0)
+    forward_last(3)
+    attend_rest(0)
+    for k in range(4):
+        multiply(3, k)
+    round_values(3)
+    attend_first(1)
+    attend_rest(1)
 
     @pl.when(is_temporal)
     def _():
-        temporal_all()
-        for r in range(1, 8):
-            back_temporal(r).start()
-        back[me % half, :, pl.ds(width, width)] = xg_ref[0, :, pl.ds(3 * width, width)]
         bias_copy().wait_send()
-        back_spatial().wait_recv()
-
-    for q in range(half):
-        @pl.when(me != half + q)
-        def _():
-            back_came(q).wait_recv()
+
+    for g in range(2):
+        @pl.when(is_temporal)
+        def _():
+            back_spatial(g).wait_recv()
+
+        for q in range(half):
+            @pl.when(me != half + q)
+            def _():
+                back_came(g, q).wait_recv()
 
     for h in range(heads):
         ranks = [n for n in range(kept) if n <= h <= n + kept]
@@ -536,15 +604,20 @@
         res = chosen_sum((heads + h) * heads, blocks)
         out_ref[:, :, pl.ds(h * HD, HD)] = res.reshape(half, quarter, HD)
 
-    @pl.when(is_spatial)
-    def _():
-        back_spatial().wait_send()
-
-    @pl.when(is_temporal)
-    def _():
-        for r in range(1, 8):
-            back_temporal(r).wait_send()
-
+    for g in range(2):
+        @pl.when(is_spatial)
+        def _():
+            back_spatial(g).wait_send()
+
+        @pl.when(is_temporal)
+        def _():
+            for r in range(1, 8):
+                back_temporal(g, r).wait_send()
+
+    for r in range(8):
+        near_copy(r).wait_send()
+        core_copy(r).wait_send()
+        pass_copy(r).wait_send()
     for r in range(8):
         sum_copy(r).wait_send()
     for p in range(3):
@@ -558,18 +631,8 @@
         def _():
             to_spatial(j).wait_send()
 
-    for i in range(kinds):
-        mate_copy(i).wait_send()
-        cross_copy(i).wait_send()
-
-        @pl.when(inner)
-        def _():
-            fwd_copy(i).wait_send()
-            a1_copy(i).wait_send()
-            a2_copy(i).wait_send()
-
-        for k in range(4):
-            y_copy(i, k).wait_send()
+    for c in range(1, 4):
+        sent_w(c)
 
 
 def attend_block(masks, x_quarters, w_qkv, gains, bias, seq_count, fsdp_count):
@@ -606,9 +669,9 @@
         ]
         + [dma((8,))] * 8
         + [dma((3,))] * 2
-        + [dma((kinds,))] * 9
-        + [dma((kinds, 4)), dma((kinds, 4)), dma((8,)), dma((8,)), dma((half,))]
-        + [dma, dma, dma((8,)), dma((8,))],
+        + [dma((kinds + 1,))] * 9
+        + [dma((kinds + 1, 4)), dma((kinds + 1, 4)), dma((8,)), dma((8,)), dma((half,))]
+        + [dma, dma, dma((2, 8)), dma((2, 8))],
         compiler_params=pltpu.CompilerParams(
             collective_id=0, has_side_effects=True, vmem_limit_bytes=61 * 1024 * 1024
         ),

time: 338 us -> 317 us (0.938)
  Pallas kernels: 324 us -> 306 us
    pallas_call x1, Pallas kernels: 324 us -> 306 us  [attend_block(): pl.pallas_call(block_kernel, out_shape=jax.ShapeDtypeStruct((half, quarte...]
where the time goes in v5:
time: 317 us; the launch traced here: 315 us
  Pallas kernels  306 us (97%)
  local copies, waits for them, and re-layouts  6.74 us (2%)
    pallas_call x1, Pallas kernels, attend_block(): pl.pallas_call(block_kernel, out_shape=jax.ShapeDtypeStruct((half, quarte...  306 us

profile of v5, /device:TPU:12, one launch (start us, length us, event | category | flops | bytes accessed | tf_op | source)
XLA Modules:
  0.0 315.4 jit_solution(9107368470007157907)
XLA Ops:
  0.0 0.7 compare_convert_fusion
  0.7 0.1 select_reduce_fusion.4
  0.8 0.7 compare_select_fusion.1
  1.5 0.1 select_reduce_fusion.3
  1.6 0.1 select_reduce_fusion.2
  1.7 0.1 pad_add_fusion
  1.7 0.1 iota_compare_fusion.4
  1.8 0.1 iota_compare_fusion.5
  1.9 0.7 stack.9
  2.6 0.7 stack.10
  3.3 0.1 select_reduce_fusion.1
  3.4 0.6 copy.10.gain_ref
  4.0 0.1 fusion
  4.1 0.1 reshape.102
  4.2 0.7 convert_element_type.22
  5.0 0.1 select_reduce_fusion
  5.1 0.1 broadcast_in_dim.115
  5.2 0.6 pad.4.bias_ref
  5.8 1.2 broadcast_in_dim.105.mask_ref
  7.0 305.7 %shard_map.64 = bf16[4,160,1280]{2,1,0:T(8,128)(2,1)} custom-call(bf16[200,16,128]{2,1,0:T(8,128)(2,1)} %broadcast_in_dim.105.mask_ref, bf16[4,160,1280]{2,1,0:T(8,128)(2,1)} %bitcast.11, bf16[3,640,1280]{2,1,0:T(8,128)(2,1)} %w_ref.1, f32[2,1,640]{2,1,0:T(1,128)} %copy.10.gain_ref, f32[5,8,640]{2,1,0:T(8,128)} %pad.4.bias_ref), custom_call_target="tpu_custom_call" | custom-call | tf_op jit(solution)/shard_map/pallas_call | solution.py:647
  312.7 2.7 copy.15
  (5 shorter events, 0.1 us)

commit v6 on v5

--- a/solution.py
+++ b/solution.py
@@ -379,10 +379,12 @@
         for k in range(4):
             y_copy(c, k).wait_send()
 
-    for k in range(3):
+    multiply(0, 0)
+    multiply(1, 0)
+    forward_w(2)
+    for k in range(1, 3):
         multiply(0, k)
         multiply(1, k)
-    forward_w(2)
     multiply(0, 3)
     multiply(1, 3)
 

time: 317 us -> 316 us (level)
  no operation moved by 1% of the time
where the time goes in v6:
time: 316 us; the launch traced here: 315 us
  Pallas kernels  305 us (97%)
  local copies, waits for them, and re-layouts  6.74 us (2%)
    pallas_call x1, Pallas kernels, attend_block(): pl.pallas_call(block_kernel, out_shape=jax.ShapeDtypeStruct((half, quarte...  305 us

profile of v6, /device:TPU:12, one launch (start us, length us, event | category | flops | bytes accessed | tf_op | source)
XLA Modules:
  0.0 314.9 jit_solution(13465214914680890726)
XLA Ops:
  0.0 0.7 compare_convert_fusion
  0.7 0.1 select_reduce_fusion.4
  0.8 0.7 compare_select_fusion.1
  1.5 0.1 select_reduce_fusion.3
  1.6 0.1 select_reduce_fusion.2
  1.7 0.1 pad_add_fusion
  1.7 0.1 iota_compare_fusion.4
  1.8 0.1 iota_compare_fusion.5
  1.9 0.7 stack.9
  2.6 0.7 stack.10
  3.3 0.1 select_reduce_fusion.1
  3.4 0.6 copy.10.gain_ref
  4.0 0.1 fusion
  4.1 0.1 reshape.102
  4.2 0.7 convert_element_type.22
  5.0 0.1 select_reduce_fusion
  5.1 0.1 broadcast_in_dim.115
  5.2 0.6 pad.4.bias_ref
  5.8 1.2 broadcast_in_dim.105.mask_ref
  7.0 305.1 %shard_map.64 = bf16[4,160,1280]{2,1,0:T(8,128)(2,1)} custom-call(bf16[200,16,128]{2,1,0:T(8,128)(2,1)} %broadcast_in_dim.105.mask_ref, bf16[4,160,1280]{2,1,0:T(8,128)(2,1)} %bitcast.11, bf16[3,640,1280]{2,1,0:T(8,128)(2,1)} %w_ref.1, f32[2,1,640]{2,1,0:T(1,128)} %copy.10.gain_ref, f32[5,8,640]{2,1,0:T(8,128)} %pad.4.bias_ref), custom_call_target="tpu_custom_call" | custom-call | tf_op jit(solution)/shard_map/pallas_call | solution.py:649
  312.2 2.7 copy.15
  (5 shorter events, 0.1 us)
